TPU v7x, 32 devices: a whole 2x2x4 slice. The times are simulated.
32 devices in a mesh: grp: 2 (over y), wide: 8 (over z, x), tp: 2 (over core).
Axes of the slice: x: 2, y: 2, z: 4, core: 2. Of those that a mesh axis runs over, the one named last changes fastest.
Arguments:
- hidden: bfloat16 [64, 4096], P(('grp', 'wide')), parts along dimension 0, may hold values from -6 to 6
- residual: bfloat16 [64, 4096], P(('grp', 'wide'), 'tp'), parts along dimension 0, may hold values from -6 to 6
- output_weight: bfloat16 [4096, 4096], P('wide', 'tp'), may hold values from -0.09375 to 0.09375
- adapter_down_factor: bfloat16 [64, 64, 4096], P('wide', None, 'tp'), may hold values from -0.09375 to 0.09375
- adapter_up_factor: bfloat16 [64, 64, 4096], P('wide', None, 'tp'), may hold values from -0.75 to 0.75
- gain: float32 [4096], P('tp'), may hold values from 0.4 to 1.6
- block_request_rows: int32 [32, 4], P(('grp', 'wide')), parts along dimension 0, may hold values from 0 to 32, as said below
- adapter_of_block: int32 [32], P(('grp', 'wide')), parts along dimension 0, may hold values from 0 to 63, as said below
Outputs:
- new_residual: bfloat16 [64, 4096], P(('grp', 'wide'), 'tp'), parts along dimension 0
- normed: bfloat16 [64, 4096], P(('grp', 'wide'), 'tp'), parts along dimension 0
There are 2 independent parts, one for each index of `grp`. A program takes and returns all parts, laid end to end along the dimension named above; an argument that names none is the same for every part. Nothing has to cross between parts.
Inputs may be any that keep to these rules, and one draw needn't show every extreme that they name: `block_request_rows`: each request index of 0 to 31 stands in exactly one slot; unused slots hold 32 and follow the used ones in their row; some block is full and some is empty. `adapter_of_block`: block b names an adapter held by the same index of wide: between (b // 2) * 8 and that plus 8 - 1; an adapter may have several blocks or none.
All inputs are finite; a program needn't handle non-finite values.
Results may differ from a plain program's by a relative error of at most 0.0033.
Values may be sent and summed in bfloat16 or wider, within the bound.
No kernel may reach another device: no remote copies, remote signals or barrier semaphores. Data moves between devices by JAX's collectives and lax.ppermute only.
A program may use at most 64 MiB of HBM per device.

v0:
```python
import jax
import jax.numpy as jnp
from jax import lax
from jax.sharding import PartitionSpec as P

epsilon = 1e-06


def adapter_update(
    request_half_rows, adapter_down_factor, adapter_up_factor, block_request_rows, adapter_of_block
):
    half_width = request_half_rows.shape[1]
    local_request_ids = adapter_of_block - lax.axis_index("wide") * adapter_down_factor.shape[0]
    selected_down = jnp.take(adapter_down_factor, local_request_ids, axis=0)
    selected_up = jnp.take(adapter_up_factor, local_request_ids, axis=0)
    padded_rows = jnp.concatenate(
        [request_half_rows, jnp.zeros((1, half_width), request_half_rows.dtype)], axis=0
    )
    picked = jnp.take(padded_rows, block_request_rows, axis=0)
    inner_part = jnp.einsum(
        "bsd,brd->bsr", picked, selected_down, preferred_element_type=jnp.float32
    )
    inner = lax.psum(inner_part, "tp").astype(jnp.bfloat16)
    update_term = jnp.einsum("bsr,brd->bsd", inner, selected_up, preferred_element_type=jnp.float32)
    return update_term.reshape(-1, half_width)


def local(
    hidden,
    residual,
    output_weight,
    adapter_down_factor,
    adapter_up_factor,
    gain,
    block_request_rows,
    adapter_of_block,
):
    width = hidden.shape[1]
    half_width = width // lax.axis_size("tp")
    core_index = lax.axis_index("tp")
    feature_count = output_weight.shape[0]
    gathered = lax.all_gather(hidden, "wide", axis=0, tiled=True)
    own_features = lax.dynamic_slice_in_dim(
        gathered, lax.axis_index("wide") * feature_count, feature_count, 1
    )
    request_half_rows = lax.dynamic_slice_in_dim(gathered, core_index * half_width, half_width, 1)
    partial_value = jnp.dot(own_features, output_weight, preferred_element_type=jnp.float32)
    update_term = adapter_update(
        request_half_rows,
        adapter_down_factor,
        adapter_up_factor,
        block_request_rows,
        adapter_of_block,
    )
    partial_value = partial_value.at[block_request_rows.reshape(-1)].add(update_term, mode="drop")
    summed_part = lax.psum_scatter(partial_value, "wide", scatter_dimension=0, tiled=True)
    summed = residual.astype(jnp.float32) + summed_part
    squares = lax.psum(jnp.sum(summed * summed, axis=1, keepdims=True), "tp")
    normed = summed * lax.rsqrt(squares / width + epsilon) * gain
    return (summed.astype(jnp.bfloat16), normed.astype(jnp.bfloat16))


def solution(mesh):
    return jax.shard_map(
        local,
        mesh=mesh,
        in_specs=(
            P(("grp", "wide"), None),
            P(("grp", "wide"), "tp"),
            P("wide", "tp"),
            P("wide", None, "tp"),
            P("wide", None, "tp"),
            P("tp"),
            P(("grp", "wide"), None),
            P(("grp", "wide")),
        ),
        out_specs=(P(("grp", "wide"), "tp"), P(("grp", "wide"), "tp")),
        check_vma=False,
    )
```

profile of v0, /device:TPU:0, one launch (start us, length us, event | category | flops | bytes accessed | tf_op | source)
XLA Modules:
  0.0 136.7 jit_solution(1911771499608333887)
XLA Ops:
  7.2 0.0 copy-start
  7.2 0.0 all-reduce.4.cloned.1.call-start
  7.2 0.8 compare_select_fusion
  8.1 0.7 compare_and_fusion.1
  8.7 0.8 reshape.49
  9.5 32.7 %all-gather = bf16[8,4,4096]{2,1,0:T(4,128)(2,1)S(1)} all-gather(bf16[1,4,4096]{2,1,0:T(4,128)(2,1)} %bitcast.9), channel_id=1, replica_groups=mesh['grp'=2,'wide'=8,'tp'=2] {'wide'}, dimensions={0}, use_global_device_ids=true | all-gather | bytes 294912 | tf_op jit(solution)/shard_map/all_gather | solution.py:42
  42.2 0.1 reshape.88
  42.3 0.1 reshape.69
  42.4 0.6 gather_fusion
  43.0 0.7 compare_and_fusion
  43.7 0.0 copy-done
  43.7 0.6 gather_fusion.1
  44.3 0.3 fusion.2
  44.6 2.5 %psum.14 = bf16[2,4,64]{2,1,0:T(4,128)(2,1)S(1)} all-reduce(f32[2,4,64]{2,1,0:T(4,128)S(1)} %fusion.2), channel_id=1, replica_groups=mesh['grp'=2,'wide'=8,'tp'=2] {'tp'}, use_global_device_ids=true, to_apply=%region_0.0 | all-reduce | flops 512 | bytes 3072 | tf_op jit(solution)/shard_map/psum | solution.py:23
  47.1 2.2 %gather_fusion.2 = bf16[2,64,2048]{2,1,0:T(8,128)(2,1)S(1)} fusion(bf16[8,64,2048]{2,1,0:T(8,128)(2,1)} %param.14, s32[1024]{0:T(1024)S(1)} %pad_clamp_fusion), kind=kCustom, calls=%fused_computation.1.clone | custom fusion | bytes 1048584 | tf_op jit(solution)/shard_map/jit(_take)/gather | solution.py:15
  49.2 0.3 fusion
  49.5 0.0 copy-start.4
  49.5 0.0 copy-start.2
  49.5 0.0 copy-start.3
  49.6 2.1 %fusion.9 = f32[32,2048]{1,0:T(8,128)S(1)} fusion(bf16[512,2048]{1,0:T(8,128)(2,1)} %param.12, bf16[32,4096]{1,0:T(8,128)(2,1)S(1)} %reshape.88, s32[]{:T(128)S(6)} %select_n.32), kind=kOutput, calls=%fused_computation.16 | convolution fusion | flops 67108864 | bytes 2392068 | tf_op jit(solution)/shard_map/dot_general | solution.py:47
  51.6 0.8 scatter_fusion
  52.5 0.0 copy-start.1
  52.5 0.7 copy-done.1
  53.2 0.0 all-reduce.4.cloned.1.call-update
  53.2 0.0 copy-done.4
  53.2 0.6 dynamic-slice
  54.4 70.4 %all-reduce.4.cloned.1.call-done = f32[32,2048]{1,0:T(8,128)} async-done(((f32[32,2048]{1,0:T(8,128)}), f32[32,2048]{1,0:T(8,128)}) %all-reduce.4.cloned.1.call-update) | async-done | bytes 262160
  124.9 0.0 copy-done.2
  124.9 1.0 multiply_reduce_fusion
  125.8 2.5 %psum.15 = f32[4,1]{0,1:T(1,128)S(1)} all-reduce(f32[4,1]{0,1:T(1,128)S(1)} %bitcast.10), channel_id=1, replica_groups=mesh['grp'=2,'wide'=8,'tp'=2] {'tp'}, use_global_device_ids=true, to_apply=%region_4.6 | all-reduce | flops 4 | bytes 32 | tf_op jit(solution)/shard_map/psum | solution.py:58
  128.3 0.0 copy-done.3
  128.3 1.5 %multiply_convert_fusion = (bf16[4,2048]{1,0:T(4,128)(2,1)}, bf16[4,2048]{1,0:T(4,128)(2,1)}) fusion(f32[2048]{0:T(1024)S(1)} %copy-done.3, f32[4]{0:T(128)S(1)} %rsqrt_bitcast_fusion, f32[32,2048]{1,0:T(8,128)} %all-reduce.4.cloned.1.call-done, u32[]{:T(128)S(6)} %multiply.2, bf16[4,2048]{1,0:T(4,128)(2,1)S(1)} %copy-done.2), kind=kLoop, calls=%fused_computation.13 | loop fusion | flops 49152 | bytes 90132 | tf_op jit(solution)/shard_map/convert_element_type | solution.py:60
  (8 shorter events, 0.1 us)
Async XLA Ops:
  7.2 36.5 %copy-start = (bf16[8,64,2048]{2,1,0:T(8,128)(2,1)S(1)}, bf16[8,64,2048]{2,1,0:T(8,128)(2,1)}, u32[]{:S(2)}) copy-start(bf16[8,64,2048]{2,1,0:T(8,128)(2,1)} %param.13) | copy-start | bytes 6291460
  7.2 117.7 %all-reduce.4.cloned.1.call-start = ((), (), s32[]{:S(2)}) async-start(), calls=%async_computation | async-start | bytes 524288
  49.5 3.7 %copy-start.4 = (u32[32]{0:T(128)S(1)}, u32[32]{0:T(128)}, u32[]{:S(2)}) copy-start(u32[32]{0:T(128)} %constant.62) | copy-start | bytes 388
  49.5 75.4 %copy-start.2 = (bf16[4,2048]{1,0:T(4,128)(2,1)S(1)}, bf16[4,2048]{1,0:T(4,128)(2,1)}, u32[]{:S(2)}) copy-start(bf16[4,2048]{1,0:T(4,128)(2,1)} %param.11) | copy-start | bytes 49156
  49.5 78.8 %copy-start.3 = (f32[2048]{0:T(1024)S(1)}, f32[2048]{0:T(1024)}, u32[]{:S(2)}) copy-start(f32[2048]{0:T(1024)} %param.15) | copy-start | bytes 24580
  52.5 0.7 copy-start.1
Sparse Core Ops, SparseCore 0:
  53.3 71.5 all-reduce.3
where the time goes:
time: 137 us
  waiting for transfers between devices  70.5 us (51%)
  blocking collectives  37.6 us (27%)
  between operations  14.8 us (11%)
  local copies, waits for them, and re-layouts  5.6 us (4%)
  other arithmetic  5.52 us (4%)
  matrix products  2.62 us (2%)
    unnamed x2, waiting for transfers between devices  70.5 us
    all_gather x1, blocking collectives, local(): gathered = lax.all_gather(hidden, 'wide', axis=0, tiled=True)  32.7 us
  transfers between devices with their start and end apart: 1, of which 1 were waited for; matrix products, arithmetic and copies ran while one was open for 0% of the time, Pallas kernels for 0%

commit v1 on v0

v1 whole, which is shorter than its diff:
```python
import jax
import jax.numpy as jnp
from jax import lax
from jax.sharding import PartitionSpec as P

epsilon = 1e-06


def local(
    hidden,
    residual,
    output_weight,
    adapter_down_factor,
    adapter_up_factor,
    gain,
    block_request_rows,
    adapter_of_block,
):
    rows, width = hidden.shape
    half_width = residual.shape[1]
    wide = lax.axis_size("wide")
    requests = wide * rows
    feature_count = output_weight.shape[0]
    adapters_here, rank, _ = adapter_down_factor.shape
    blocks = adapter_of_block.shape[0]
    core = lax.axis_index("tp")
    swap = [(0, 1), (1, 0)]

    ids = adapter_of_block - lax.axis_index("wide") * adapters_here
    selected_down = jnp.take(adapter_down_factor, ids, axis=0, mode="clip").reshape(blocks * rank, half_width)
    selected_up = jnp.take(adapter_up_factor, ids, axis=0, mode="clip").reshape(blocks * rank, half_width)

    half = lax.dynamic_slice_in_dim(hidden, core * half_width, half_width, 1)
    columns = hidden.reshape(rows, wide, feature_count).transpose(1, 0, 2)
    sent = jnp.concatenate(
        [jnp.broadcast_to(half[None], (wide, rows, half_width)), columns], axis=2
    )
    received = lax.all_to_all(sent, "wide", 0, 0).reshape(requests, half_width + feature_count)
    half_rows = received[:, :half_width]
    own_features = received[:, half_width:]

    inner_part = lax.dot_general(
        half_rows, selected_down, (((1,), (1,)), ((), ())), preferred_element_type=jnp.float32
    )
    inner_other = lax.ppermute(inner_part, "tp", swap)
    inner = (inner_part + inner_other).astype(jnp.bfloat16)
    request_index = lax.broadcasted_iota(jnp.int32, (requests, blocks), 0)
    holds = jnp.any(request_index[:, :, None] == block_request_rows[None], axis=2)
    inner = jnp.where(jnp.repeat(holds, rank, axis=1), inner, jnp.zeros_like(inner))

    partial_value = jnp.dot(own_features, output_weight, preferred_element_type=jnp.float32)
    partial_value += jnp.dot(inner, selected_up, preferred_element_type=jnp.float32)
    terms = lax.all_to_all(
        partial_value.astype(jnp.bfloat16).reshape(wide, rows, half_width), "wide", 0, 0
    )
    summed = residual.astype(jnp.float32) + jnp.sum(terms.astype(jnp.float32), axis=0)
    squares = jnp.sum(summed * summed, axis=1, keepdims=True)
    squares += lax.ppermute(squares, "tp", swap)
    normed = summed * lax.rsqrt(squares / width + epsilon) * gain
    return (summed.astype(jnp.bfloat16), normed.astype(jnp.bfloat16))


def solution(mesh):
    return jax.shard_map(
        local,
        mesh=mesh,
        in_specs=(
            P(("grp", "wide"), None),
            P(("grp", "wide"), "tp"),
            P("wide", "tp"),
            P("wide", None, "tp"),
            P("wide", None, "tp"),
            P("tp"),
            P(("grp", "wide"), None),
            P(("grp", "wide")),
        ),
        out_specs=(P(("grp", "wide"), "tp"), P(("grp", "wide"), "tp")),
        check_vma=False,
    )
```

time: 137 us -> 33.4 us (0.24)
  waiting for transfers between devices: 70.5 us -> 4.84 us
  blocking collectives: 37.6 us -> 10.3 us
  between operations: 14.8 us -> 0.77 us
  starting transfers between devices: 0.04 us -> 7.39 us
  other arithmetic: 5.52 us -> 2.38 us
    unnamed x2 -> x0, waiting for transfers between devices: 70.5 us -> none
    all_gather x1 -> x0, blocking collectives: 32.7 us -> none  [local(): gathered = lax.all_gather(hidden, 'wide', axis=0, tiled=True)]
    all_to_all x0 -> x1, blocking collectives: none -> 10.3 us  [local(): lax.all_to_all(partial_value.astype(jnp.bfloat16).reshape(wide, rows, hal...]
    all_to_all x0 -> x1, starting transfers between devices: none -> 7.25 us  [local(): lax.all_to_all(sent, 'wide', 0, 0)]
    psum x2 -> x0, blocking collectives: 4.92 us -> none  [the longest x1 2.46 us: local(): squares = lax.psum(jnp.sum(summed * summed, axis=1, keepdims=True), 'tp')]
    all_to_all x0 -> x1, waiting for transfers between devices: none -> 3.72 us  [local(): lax.all_to_all(sent, 'wide', 0, 0)]
    gather x4 -> x2, local copies, waits for them, and re-layouts: 3.35 us -> 2.75 us  [the longest x1 2.17 us: local(): jnp.take(adapter_up_factor, ids, axis=0, mode='clip')]
  transfers between devices with their start and end apart: 1 -> 3, of which waited for: 1 -> 2; matrix products, arithmetic and copies ran while one was open for 0% -> 18% of each run, Pallas kernels for 0% -> 0%
where the time goes in v1:
time: 33.4 us; the launch traced here: 33.1 us
  blocking collectives  10.3 us (31%)
  starting transfers between devices  7.39 us (22%)
  local copies, waits for them, and re-layouts  4.87 us (15%)
  waiting for transfers between devices  4.84 us (14%)
  matrix products  2.52 us (8%)
  other arithmetic  2.38 us (7%)
  between operations  0.77 us (2%)
    all_to_all x1, blocking collectives, local(): lax.all_to_all(partial_value.astype(jnp.bfloat16).reshape(wide, rows, hal...  10.3 us
    all_to_all x1, starting transfers between devices, local(): lax.all_to_all(sent, 'wide', 0, 0)  7.25 us
    all_to_all x1, waiting for transfers between devices, local(): lax.all_to_all(sent, 'wide', 0, 0)  3.72 us
    gather x1, local copies, waits for them, and re-layouts, local(): jnp.take(adapter_up_factor, ids, axis=0, mode='clip')  2.17 us
    dot_general x1, matrix products, local(): jnp.dot(own_features, output_weight, preferred_element_type=jnp.float32)  2.06 us
    ppermute x1, waiting for transfers between devices, local(): squares += lax.ppermute(squares, 'tp', swap)  1.11 us
    dynamic_slice x1, local copies, waits for them, and re-layouts, local(): half = lax.dynamic_slice_in_dim(hidden, core * half_width, half_width, 1)  0.87 us
    unnamed x9, local copies, waits for them, and re-layouts  0.79 us
  transfers between devices with their start and end apart: 3, of which 2 were waited for; matrix products, arithmetic and copies ran while one was open for 18% of the time, Pallas kernels for 0%

profile of v1, /device:TPU:0, one launch (start us, length us, event | category | flops | bytes accessed | tf_op | source)
XLA Modules:
  0.0 33.1 jit_solution(13857789708164378212)
XLA Ops:
  0.6 0.0 copy-start
  0.6 0.0 copy-start.3
  0.7 0.9 %constant_dynamic-slice_fusion = bf16[4,2048]{1,0:T(4,128)(2,1)S(1)} fusion(bf16[4,4096]{1,0:T(4,128)(2,1)} %param.8, s32[]{:T(128)S(6)} %select_n.7), kind=kLoop, calls=%fused_computation.23 | loop fusion | bytes 32772 | tf_op jit(solution)/shard_map/dynamic_slice | solution.py:33
  1.5 0.8 %copy.16 = bf16[1,4,8,512]{3,2,1,0:T(8,128)(2,1)S(1)} copy(bf16[1,4,8,512]{3,1,2,0:T(4,128)(2,1)} %bitcast.19) | data formatting | bytes 65536
  2.4 0.7 %pad_maximum_fusion = bf16[8,4,2560]{2,1,0:T(4,128)(2,1)} fusion(bf16[8,4,512]{2,1,0:T(4,128)(2,1)S(1)} %copy.12, bf16[8,4,2048]{2,1,0:T(4,128)(2,1)S(1)} %broadcast_in_dim.23), kind=kLoop, calls=%fused_computation.5 | loop fusion | flops 327680 | bytes 327680 | tf_op jit(solution)/shard_map/concatenate | solution.py:35
  3.1 7.3 %all-to-all-start = ((bf16[8,4,2560]{2,1,0:T(4,128)(2,1)}), bf16[8,4,2560]{2,1,0:T(4,128)(2,1)S(1)}, u32[]{:S(2)}, u32[]{:S(2)}) async-start(bf16[8,4,2560]{2,1,0:T(4,128)(2,1)} %pad_maximum_fusion), calls=%async_computation | async-start | bytes 327680 | tf_op jit(solution)/shard_map/all_to_all | solution.py:38
  10.4 0.7 %broadcast_subtract_fusion = s32[2]{0:T(128)S(1)} fusion(s32[2]{0:T(128)} %param.15, s32[]{:T(128)S(6)} %mul.28), kind=kLoop, calls=%fused_computation.22 | loop fusion | flops 2 | bytes 20 | tf_op jit(solution)/shard_map/sub | solution.py:29
  11.0 0.0 copy-done
  11.0 0.6 %gather_fusion = bf16[2,64,2048]{2,1,0:T(8,128)(2,1)S(1)} fusion(bf16[8,64,2048]{2,1,0:T(8,128)(2,1)S(1)} %copy-done, s32[1024]{0:T(1024)S(1)} %pad_clamp_fusion), kind=kCustom, calls=%fused_computation | custom fusion | bytes 1048584 | tf_op jit(solution)/shard_map/jit(_take)/gather | solution.py:30
  11.6 2.2 %gather_fusion.1 = bf16[2,64,2048]{2,1,0:T(8,128)(2,1)S(1)} fusion(bf16[8,64,2048]{2,1,0:T(8,128)(2,1)} %param.12, s32[1024]{0:T(1024)S(1)} %pad_clamp_fusion), kind=kCustom, calls=%fused_computation.1 | custom fusion | bytes 1048584 | tf_op jit(solution)/shard_map/jit(_take)/gather | solution.py:31
  13.8 0.0 copy-done.3
  13.8 0.1 fusion.9
  13.9 0.1 copy.13
  14.0 0.1 broadcast_in_dim.24
  14.1 0.1 reshape.27
  14.2 3.7 %all-to-all-done = bf16[8,4,2560]{2,1,0:T(4,128)(2,1)S(1)} async-done(((bf16[8,4,2560]{2,1,0:T(4,128)(2,1)}), bf16[8,4,2560]{2,1,0:T(4,128)(2,1)S(1)}, u32[]{:S(2)}, u32[]{:S(2)}) %all-to-all-start) | async-done | bytes 163872 | tf_op jit(solution)/shard_map/all_to_all | solution.py:38
  18.0 0.3 fusion.1
  18.2 0.0 copy-start.1
  18.2 0.0 copy-start.2
  18.3 0.1 collective-permute-start
  18.3 2.1 %fusion.3 = f32[32,2048]{1,0:T(8,128)S(1)} fusion(bf16[512,2048]{1,0:T(8,128)(2,1)} %param.10, bf16[32,2560]{1,0:T(8,128)(2,1)S(1)} %reshape.26), kind=kOutput, calls=%fused_computation.9 | convolution fusion | flops 67108864 | bytes 2392064 | tf_op jit(solution)/shard_map/dot_general | solution.py:51
  20.4 0.0 collective-permute-done
  20.4 0.2 fusion
  20.6 0.1 reshape.30
  20.7 10.3 %all_to_all.10 = bf16[8,4,2048]{2,1,0:T(4,128)(2,1)S(1)} all-to-all(bf16[8,4,2048]{2,1,0:T(4,128)(2,1)S(1)} %reshape.30), channel_id=1, replica_groups=mesh['grp'=2,'wide'=8,'tp'=2] {'wide'}, dimensions={0} | all-to-all | bytes 262144 | tf_op jit(solution)/shard_map/all_to_all | solution.py:53
  31.0 0.1 convert_reduce_fusion
  31.1 0.0 copy-done.1
  31.1 0.1 multiply_reduce_fusion
  31.2 0.1 collective-permute-start.1
  31.3 1.1 %collective-permute-done.1 = f32[4,1]{0,1:T(1,128)S(1)} collective-permute-done((f32[4,1]{0,1:T(1,128)S(1)}, f32[4,1]{0,1:T(1,128)S(1)}, u32[]{:S(2)}, u32[]{:S(2)}) %collective-permute-start.1) | collective-permute-done | bytes 48 | tf_op jit(solution)/shard_map/ppermute | solution.py:58
  32.4 0.0 copy-done.2
  32.4 0.7 %multiply_convert_fusion = (bf16[4,2048]{1,0:T(4,128)(2,1)}, bf16[4,2048]{1,0:T(4,128)(2,1)}) fusion(f32[2048]{0:T(1024)S(1)} %copy-done.2, f32[4]{0:T(128)S(1)} %rsqrt_bitcast_fusion, f32[4,2048]{1,0:T(4,128)S(1)} %convert_reduce_fusion, bf16[4,2048]{1,0:T(4,128)(2,1)S(1)} %copy-done.1), kind=kLoop, calls=%fused_computation.11 | loop fusion | flops 49152 | bytes 90128 | tf_op jit(solution)/shard_map/convert_element_type | solution.py:60
  (5 shorter events, 0.1 us)
Async XLA Ops:
  0.6 10.4 %copy-start = (bf16[8,64,2048]{2,1,0:T(8,128)(2,1)S(1)}, bf16[8,64,2048]{2,1,0:T(8,128)(2,1)}, u32[]{:S(2)}) copy-start(bf16[8,64,2048]{2,1,0:T(8,128)(2,1)} %param.11) | copy-start | bytes 6291460
  0.6 13.1 %copy-start.3 = (s32[2,4]{1,0:T(2,128)S(1)}, s32[2,4]{1,0:T(2,128)}, u32[]{:S(2)}) copy-start(s32[2,4]{1,0:T(2,128)} %param.14) | copy-start | bytes 100
  3.1 14.8 %all-to-all-start = ((bf16[8,4,2560]{2,1,0:T(4,128)(2,1)}), bf16[8,4,2560]{2,1,0:T(4,128)(2,1)S(1)}, u32[]{:S(2)}, u32[]{:S(2)}) async-start(bf16[8,4,2560]{2,1,0:T(4,128)(2,1)} %pad_maximum_fusion), calls=%async_computation | async-start | bytes 327680 | tf_op jit(solution)/shard_map/all_to_all | solution.py:38
  18.2 12.8 %copy-start.1 = (bf16[4,2048]{1,0:T(4,128)(2,1)S(1)}, bf16[4,2048]{1,0:T(4,128)(2,1)}, u32[]{:S(2)}) copy-start(bf16[4,2048]{1,0:T(4,128)(2,1)} %param.9) | copy-start | bytes 49156
  18.2 14.1 %copy-start.2 = (f32[2048]{0:T(1024)S(1)}, f32[2048]{0:T(1024)}, u32[]{:S(2)}) copy-start(f32[2048]{0:T(1024)} %param.13) | copy-start | bytes 24580
  18.3 2.1 %collective-permute-start = (f32[32,128]{1,0:T(8,128)S(1)}, f32[32,128]{1,0:T(8,128)S(1)}, u32[]{:S(2)}, u32[]{:S(2)}) collective-permute-start(f32[32,128]{1,0:T(8,128)S(1)} %fusion.1), channel_id=1, source_target_pairs={{0,1},{1,0},{2,3},{3,2},{4,5},{5,4},{6,7},{7,6},{8,9},{9,8},{10,11... | collective-permute-start | bytes 49160 | tf_op jit(solution)/shard_map/ppermute | solution.py:45
  31.2 1.2 %collective-permute-start.1 = (f32[4,1]{0,1:T(1,128)S(1)}, f32[4,1]{0,1:T(1,128)S(1)}, u32[]{:S(2)}, u32[]{:S(2)}) collective-permute-start(f32[4,1]{0,1:T(1,128)S(1)} %bitcast.20), channel_id=1, source_target_pairs={{0,1},{1,0},{2,3},{3,2},{4,5},{5,4},{6,7},{7,6},{8,9},{9,8},{10,11... | collective-permute-start | bytes 56 | tf_op jit(solution)/shard_map/ppermute | solution.py:58

commit v2 on v1

v2 whole, which is shorter than its diff:
```python
import functools

import jax
import jax.numpy as jnp
from jax import lax
from jax.experimental import pallas as pl
from jax.experimental.pallas import tpu as pltpu
from jax.sharding import PartitionSpec as P

epsilon = 1e-06
VMEM = pl.BlockSpec(memory_space=pltpu.VMEM)
SMEM = pl.BlockSpec(memory_space=pltpu.SMEM)
ANY = pl.BlockSpec(memory_space=pl.ANY)


def exchange_order(wide):
    if wide == 8:
        return [4, 1, 0, 3, 7, 2, 5, 6]
    middle = wide // 2
    return [middle] + [index for index in range(wide) if index != middle]


def pack(order, half_width, feature_count, hidden_ref, sent_ref):
    start = pl.multiple_of(lax.axis_index("tp") * half_width, 128)
    half = hidden_ref[:, pl.ds(start, half_width)]
    for place, device in enumerate(order):
        sent_ref[place, :, :half_width] = half
        sent_ref[place, :, half_width:] = hidden_ref[
            :, device * feature_count : (device + 1) * feature_count
        ]


def fetch(
    order, rows, adapters_here, ids_ref, slots_ref, down_ref, up_ref, down_out, up_out, holds_out, sems
):
    blocks, rank, _ = down_out.shape
    base = lax.axis_index("wide") * adapters_here
    copies = []
    for block in range(blocks):
        adapter = jnp.clip(ids_ref[block] - base, 0, adapters_here - 1)
        copies.append(
            pltpu.make_async_copy(down_ref.at[adapter], down_out.at[block], sems.at[2 * block])
        )
        copies.append(
            pltpu.make_async_copy(up_ref.at[adapter], up_out.at[block], sems.at[2 * block + 1])
        )
    for copy in copies:
        copy.start()
    requests = holds_out.shape[0]
    line = lax.broadcasted_iota(jnp.int32, (requests, rank), 0)
    place, within = line // rows, line % rows
    device = place
    for index, member in enumerate(order):
        if member != index:
            device = jnp.where(place == index, member, device)
    request = device * rows + within
    for block in range(blocks):
        held = request == slots_ref[block, 0]
        for slot in range(1, slots_ref.shape[1]):
            held = held | (request == slots_ref[block, slot])
        holds_out[:, block * rank : (block + 1) * rank] = held.astype(jnp.float32)
    for copy in copies:
        copy.wait()


def local(
    hidden,
    residual,
    output_weight,
    adapter_down_factor,
    adapter_up_factor,
    gain,
    block_request_rows,
    adapter_of_block,
):
    rows, width = hidden.shape
    half_width = residual.shape[1]
    wide = lax.axis_size("wide")
    requests = wide * rows
    feature_count = output_weight.shape[0]
    adapters_here, rank, _ = adapter_down_factor.shape
    blocks = adapter_of_block.shape[0]
    swap = [(0, 1), (1, 0)]
    order = exchange_order(wide)
    exchange = functools.partial(
        lax.all_to_all, axis_name="wide", split_axis=0, concat_axis=0, axis_index_groups=[order]
    )

    sent = pl.pallas_call(
        functools.partial(pack, order, half_width, feature_count),
        out_shape=jax.ShapeDtypeStruct((wide, rows, half_width + feature_count), jnp.bfloat16),
        in_specs=[VMEM],
        out_specs=VMEM,
        name="pack",
    )(hidden)
    received = exchange(sent).reshape(requests, half_width + feature_count)
    half_rows = received[:, :half_width]
    own_features = received[:, half_width:]

    factor = (blocks, rank, half_width)
    selected_down, selected_up, holds = pl.pallas_call(
        functools.partial(fetch, order, rows, adapters_here),
        out_shape=[pltpu.VMEM(factor, jnp.bfloat16)] * 2
        + [pltpu.VMEM((requests, blocks * rank), jnp.float32)],
        in_specs=[SMEM, SMEM, ANY, ANY],
        out_specs=[VMEM, VMEM, VMEM],
        scratch_shapes=[pltpu.SemaphoreType.DMA((2 * blocks,))],
        cost_estimate=pl.CostEstimate(
            flops=0, bytes_accessed=8 * blocks * rank * half_width, transcendentals=0
        ),
        name="fetch",
    )(adapter_of_block, block_request_rows, adapter_down_factor, adapter_up_factor)
    selected_down = selected_down.reshape(blocks * rank, half_width)
    selected_up = selected_up.reshape(blocks * rank, half_width)

    inner_part = lax.dot_general(
        half_rows, selected_down, (((1,), (1,)), ((), ())), preferred_element_type=jnp.float32
    )
    inner_other = lax.ppermute(inner_part, "tp", swap)
    inner = (inner_part + inner_other).astype(jnp.bfloat16)
    inner = jnp.where(holds != 0, inner, jnp.zeros_like(inner))

    partial_value = jnp.dot(own_features, output_weight, preferred_element_type=jnp.float32)
    partial_value += jnp.dot(inner, selected_up, preferred_element_type=jnp.float32)
    terms = exchange(partial_value.astype(jnp.bfloat16).reshape(wide, rows, half_width))
    summed = residual.astype(jnp.float32) + jnp.sum(terms.astype(jnp.float32), axis=0)
    squares = jnp.sum(summed * summed, axis=1, keepdims=True)
    squares += lax.ppermute(squares, "tp", swap)
    normed = summed * lax.rsqrt(squares / width + epsilon) * gain
    return (summed.astype(jnp.bfloat16), normed.astype(jnp.bfloat16))


def solution(mesh):
    return jax.shard_map(
        local,
        mesh=mesh,
        in_specs=(
            P(("grp", "wide"), None),
            P(("grp", "wide"), "tp"),
            P("wide", "tp"),
            P("wide", None, "tp"),
            P("wide", None, "tp"),
            P("tp"),
            P(("grp", "wide"), None),
            P(("grp", "wide")),
        ),
        out_specs=(P(("grp", "wide"), "tp"), P(("grp", "wide"), "tp")),
        check_vma=False,
    )
```

time: 33.4 us -> 28.8 us (0.86)
  local copies, waits for them, and re-layouts: 4.87 us -> 0.12 us
  Pallas kernels: 0 us -> 3.5 us
  matrix products: 2.52 us -> 0.93 us
  other arithmetic: 2.38 us -> 0.89 us
  blocking collectives: 10.3 us -> 9.12 us
  starting transfers between devices: 7.39 us -> 7.95 us
  waiting for transfers between devices: 4.84 us -> 5.27 us
    pallas_call x0 -> x2, Pallas kernels: none -> 3.5 us  [the longest x1 1.93 us: local(): pl.pallas_call(functools.partial(fetch, order, rows, adapters_here), out_...]
    gather x2 -> x0, local copies, waits for them, and re-layouts: 2.75 us -> none  [the longest x1 2.17 us: local(): jnp.take(adapter_up_factor, ids, axis=0, mode='clip')]
    dot_general x1, matrix products: 2.06 us -> 0.46 us  [local(): jnp.dot(own_features, output_weight, preferred_element_type=jnp.float32)]
    all_to_all x1, blocking collectives: 10.3 us -> 9.12 us  [local(): exchange(partial_value.astype(jnp.bfloat16).reshape(wide, rows, half_width))]
    dynamic_slice x1 -> x0, local copies, waits for them, and re-layouts: 0.87 us -> none  [local(): half = lax.dynamic_slice_in_dim(hidden, core * half_width, half_width, 1)]
    unnamed x9 -> x6, local copies, waits for them, and re-layouts: 0.79 us -> 0.02 us
    concatenate x1 -> x0, other arithmetic: 0.73 us -> none  [local(): jnp.concatenate([jnp.broadcast_to(half[None], (wide, rows, half_width)),...]
    ppermute x1, waiting for transfers between devices: 0.01 us -> 0.7 us  [local(): inner_other = lax.ppermute(inner_part, 'tp', swap)]
  transfers between devices with their start and end apart: 3 -> 3, of which waited for: 2 -> 3; matrix products, arithmetic and copies ran while one was open for 18% -> 2% of each run, Pallas kernels for 0% -> 7%
where the time goes in v2:
time: 28.8 us; the launch traced here: 28.5 us
  blocking collectives  9.12 us (32%)
  starting transfers between devices  7.95 us (28%)
  waiting for transfers between devices  5.27 us (18%)
  Pallas kernels  3.5 us (12%)
  matrix products  0.93 us (3%)
  other arithmetic  0.89 us (3%)
  between operations  0.72 us (2%)
    all_to_all x1, blocking collectives, local(): exchange(partial_value.astype(jnp.bfloat16).reshape(wide, rows, half_width))  9.12 us
    all_to_all x1, starting transfers between devices, local(): received = exchange(sent).reshape(requests, half_width + feature_count)  7.81 us
    all_to_all x1, waiting for transfers between devices, local(): received = exchange(sent).reshape(requests, half_width + feature_count)  3.47 us
    pallas_call x1, Pallas kernels, local(): pl.pallas_call(functools.partial(fetch, order, rows, adapters_here), out_...  1.93 us
    pallas_call x1, Pallas kernels, local(): pl.pallas_call(functools.partial(pack, order, half_width, feature_count),...  1.57 us
    ppermute x1, waiting for transfers between devices, local(): squares += lax.ppermute(squares, 'tp', swap)  1.11 us
    ppermute x1, waiting for transfers between devices, local(): inner_other = lax.ppermute(inner_part, 'tp', swap)  0.7 us
    convert_element_type x1, other arithmetic, local(): return (summed.astype(jnp.bfloat16), normed.astype(jnp.bfloat16))  0.69 us
  transfers between devices with their start and end apart: 3, of which 3 were waited for; matrix products, arithmetic and copies ran while one was open for 2% of the time, Pallas kernels for 7%

profile of v2, /device:TPU:0, one launch (start us, length us, event | category | flops | bytes accessed | tf_op | source)
XLA Modules:
  0.0 28.5 jit_solution(2620404048666087488)
XLA Ops:
  0.6 0.0 copy-start
  0.6 1.6 %pack.1 = bf16[8,4,2560]{2,1,0:T(4,128)(2,1)} custom-call(bf16[4,4096]{1,0:T(4,128)(2,1)} %hidden_ref.1), custom_call_target="tpu_custom_call" | custom-call | tf_op jit(solution)/shard_map/pack/pallas_call | solution.py:89
  2.2 7.8 %all-to-all-start = ((bf16[8,4,2560]{2,1,0:T(4,128)(2,1)}), bf16[8,4,2560]{2,1,0:T(4,128)(2,1)S(1)}, u32[]{:S(2)}, u32[]{:S(2)}) async-start(bf16[8,4,2560]{2,1,0:T(4,128)(2,1)} %pack.1), calls=%async_computation | async-start | bytes 327680 | tf_op jit(solution)/shard_map/all_to_all | solution.py:96
  10.0 1.9 %fetch.1 = (bf16[2,64,2048]{2,1,0:T(8,128)(2,1)S(1)}, bf16[2,64,2048]{2,1,0:T(8,128)(2,1)S(1)}, f32[32,128]{1,0:T(8,128)S(1)}) custom-call(s32[2]{0:T(128)} %ids_ref.1, s32[2,4]{1,0:T(2,128)} %slots_ref.1, bf16[8,64,2048]{2,1,0:T(8,128)(2,1)} %down_ref.1, bf16[8,64,2048]{2,1,0:T(8,128)(2,1)} %up_ref.1), custom_call_target="tpu_custom_call" | custom-call | bytes 2097152 | tf_op jit(solution)/shard_map/fetch/pallas_call | solution.py:101
  12.0 3.5 %all-to-all-done = bf16[8,4,2560]{2,1,0:T(4,128)(2,1)S(1)} async-done(((bf16[8,4,2560]{2,1,0:T(4,128)(2,1)}), bf16[8,4,2560]{2,1,0:T(4,128)(2,1)S(1)}, u32[]{:S(2)}, u32[]{:S(2)}) %all-to-all-start) | async-done | bytes 163872 | tf_op jit(solution)/shard_map/all_to_all | solution.py:96
  15.5 0.3 convolution_bitcast_fusion
  15.7 0.0 copy-start.1
  15.8 0.0 copy-start.2
  15.8 0.1 collective-permute-start
  15.9 0.0 copy-done
  15.9 0.5 %fusion.2 = f32[32,2048]{1,0:T(8,128)S(1)} fusion(bf16[512,2048]{1,0:T(8,128)(2,1)S(1)} %copy-done, bf16[32,2560]{1,0:T(8,128)(2,1)S(1)} %reshape.17), kind=kOutput, calls=%fused_computation.5 | convolution fusion | flops 67108864 | bytes 2392064 | tf_op jit(solution)/shard_map/dot_general | solution.py:123
  16.3 0.7 %collective-permute-done = f32[32,128]{1,0:T(8,128)S(1)} collective-permute-done((f32[32,128]{1,0:T(8,128)S(1)}, f32[32,128]{1,0:T(8,128)S(1)}, u32[]{:S(2)}, u32[]{:S(2)}) %collective-permute-start) | collective-permute-done | bytes 16416 | tf_op jit(solution)/shard_map/ppermute | solution.py:119
  17.0 0.2 fusion
  17.2 0.1 reshape.20
  17.3 9.1 %all_to_all.10 = bf16[8,4,2048]{2,1,0:T(4,128)(2,1)S(1)} all-to-all(bf16[8,4,2048]{2,1,0:T(4,128)(2,1)S(1)} %reshape.20), channel_id=1, replica_groups={{8,2,0,6,14,4,10,12},{9,3,1,7,15,5,11,13},{24,18,16,22,30,20,26,28},{25..., dimensions={0} | all-to-all | bytes 262144 | tf_op jit(solution)/shard_map/all_to_all | solution.py:125
  26.4 0.1 convert_reduce_fusion
  26.5 0.0 copy-done.1
  26.5 0.1 multiply_reduce_fusion
  26.6 0.1 collective-permute-start.1
  26.7 1.1 %collective-permute-done.1 = f32[4,1]{0,1:T(1,128)S(1)} collective-permute-done((f32[4,1]{0,1:T(1,128)S(1)}, f32[4,1]{0,1:T(1,128)S(1)}, u32[]{:S(2)}, u32[]{:S(2)}) %collective-permute-start.1) | collective-permute-done | bytes 48 | tf_op jit(solution)/shard_map/ppermute | solution.py:128
  27.8 0.0 copy-done.2
  27.8 0.7 %multiply_convert_fusion = (bf16[4,2048]{1,0:T(4,128)(2,1)}, bf16[4,2048]{1,0:T(4,128)(2,1)}) fusion(f32[2048]{0:T(1024)S(1)} %copy-done.2, f32[4]{0:T(128)S(1)} %rsqrt_bitcast_fusion, f32[4,2048]{1,0:T(4,128)S(1)} %convert_reduce_fusion, bf16[4,2048]{1,0:T(4,128)(2,1)S(1)} %copy-done.1), kind=kLoop, calls=%fused_computation.7 | loop fusion | flops 49152 | bytes 90128 | tf_op jit(solution)/shard_map/convert_element_type | solution.py:130
  (2 shorter events, 0.0 us)
Async XLA Ops:
  0.6 15.2 %copy-start = (bf16[512,2048]{1,0:T(8,128)(2,1)S(1)}, bf16[512,2048]{1,0:T(8,128)(2,1)}, u32[]{:S(2)}) copy-start(bf16[512,2048]{1,0:T(8,128)(2,1)} %param.10) | copy-start | bytes 6291460
  2.2 13.2 %all-to-all-start = ((bf16[8,4,2560]{2,1,0:T(4,128)(2,1)}), bf16[8,4,2560]{2,1,0:T(4,128)(2,1)S(1)}, u32[]{:S(2)}, u32[]{:S(2)}) async-start(bf16[8,4,2560]{2,1,0:T(4,128)(2,1)} %pack.1), calls=%async_computation | async-start | bytes 327680 | tf_op jit(solution)/shard_map/all_to_all | solution.py:96
  15.7 10.7 %copy-start.1 = (bf16[4,2048]{1,0:T(4,128)(2,1)S(1)}, bf16[4,2048]{1,0:T(4,128)(2,1)}, u32[]{:S(2)}) copy-start(bf16[4,2048]{1,0:T(4,128)(2,1)} %param.9) | copy-start | bytes 49156
  15.8 12.1 %copy-start.2 = (f32[2048]{0:T(1024)S(1)}, f32[2048]{0:T(1024)}, u32[]{:S(2)}) copy-start(f32[2048]{0:T(1024)} %param.13) | copy-start | bytes 24580
  15.8 1.2 %collective-permute-start = (f32[32,128]{1,0:T(8,128)S(1)}, f32[32,128]{1,0:T(8,128)S(1)}, u32[]{:S(2)}, u32[]{:S(2)}) collective-permute-start(f32[32,128]{1,0:T(8,128)S(1)} %convolution_bitcast_fusion), channel_id=1, source_target_pairs={{0,1},{1,0},{2,3},{3,2},{4,5},{5,4},{6,7},{7,6},{8,9},{9,8},{10,11... | collective-permute-start | bytes 49160 | tf_op jit(solution)/shard_map/ppermute | solution.py:119
  26.6 1.2 %collective-permute-start.1 = (f32[4,1]{0,1:T(1,128)S(1)}, f32[4,1]{0,1:T(1,128)S(1)}, u32[]{:S(2)}, u32[]{:S(2)}) collective-permute-start(f32[4,1]{0,1:T(1,128)S(1)} %bitcast.13), channel_id=1, source_target_pairs={{0,1},{1,0},{2,3},{3,2},{4,5},{5,4},{6,7},{7,6},{8,9},{9,8},{10,11... | collective-permute-start | bytes 56 | tf_op jit(solution)/shard_map/ppermute | solution.py:128

commit v3 on v2

v3 whole, which is shorter than its diff:
```python
import functools

import jax
import jax.numpy as jnp
from jax import lax
from jax.experimental import pallas as pl
from jax.experimental.pallas import tpu as pltpu
from jax.sharding import PartitionSpec as P

epsilon = 1e-06
VMEM = pl.BlockSpec(memory_space=pltpu.VMEM)
SMEM = pl.BlockSpec(memory_space=pltpu.SMEM)
HBM = pl.BlockSpec(memory_space=pltpu.HBM)


def in_vmem(*arrays):
    return [pltpu.with_memory_space_constraint(array, pltpu.VMEM) for array in arrays]


def in_hbm(*arrays):
    return [pltpu.with_memory_space_constraint(array, pltpu.HBM) for array in arrays]


def exchange_orders(wide):
    if wide == 8:
        return [4, 1, 0, 3, 7, 2, 5, 6], [5, 7, 3, 1, 0, 2, 6, 4]
    middle = wide // 2
    order = [middle] + [index for index in range(wide) if index != middle]
    return order, order


def pack(half_width, hidden_ref, sent_ref):
    start = pl.multiple_of(lax.axis_index("tp") * half_width, 128)
    half = hidden_ref[:, pl.ds(start, half_width)]
    for place in range(sent_ref.shape[0]):
        sent_ref[place] = half


def fetch(
    order,
    rows,
    adapters_here,
    ids_ref,
    slots_ref,
    weight_ref,
    down_ref,
    up_ref,
    weight_out,
    down_out,
    up_out,
    holds_out,
    sems,
):
    blocks, rank, _ = down_out.shape
    base = lax.axis_index("wide") * adapters_here
    copies = [pltpu.make_async_copy(weight_ref, weight_out, sems.at[2 * blocks])]
    for block in range(blocks):
        adapter = jnp.clip(ids_ref[block] - base, 0, adapters_here - 1)
        copies.append(
            pltpu.make_async_copy(down_ref.at[adapter], down_out.at[block], sems.at[2 * block])
        )
        copies.append(
            pltpu.make_async_copy(up_ref.at[adapter], up_out.at[block], sems.at[2 * block + 1])
        )
    for copy in copies:
        copy.start()
    requests = holds_out.shape[0]
    line = lax.broadcasted_iota(jnp.int32, (requests, rank), 0)
    place, within = line // rows, line % rows
    device = place
    for index, member in enumerate(order):
        if member != index:
            device = jnp.where(place == index, member, device)
    request = device * rows + within
    for block in range(blocks):
        held = request == slots_ref[block, 0]
        for slot in range(1, slots_ref.shape[1]):
            held = held | (request == slots_ref[block, slot])
        holds_out[:, block * rank : (block + 1) * rank] = held.astype(jnp.float32)
    for copy in copies:
        copy.wait()


def project(own_columns_ref, other_columns_ref, weight_ref, projected_ref):
    feature_count, half_width = weight_ref.shape
    mine = lax.axis_index("wide") * feature_count // half_width == lax.axis_index("tp")
    columns = jnp.where(mine, own_columns_ref[...], other_columns_ref[...])
    projected_ref[...] = jnp.dot(columns, weight_ref[...], preferred_element_type=jnp.float32)


def combine(
    first, second, rows, projected_ref, own_ref, other_ref, holds_ref, up_ref, sent_ref
):
    inner = (own_ref[...] + other_ref[...]).astype(jnp.bfloat16)
    inner = jnp.where(holds_ref[...] != 0, inner, jnp.zeros_like(inner))
    total = projected_ref[...] + jnp.dot(inner, up_ref[...], preferred_element_type=jnp.float32)
    for place, device in enumerate(second):
        start = first.index(device) * rows
        sent_ref[place] = total[start : start + rows].astype(sent_ref.dtype)


def local(
    hidden,
    residual,
    output_weight,
    adapter_down_factor,
    adapter_up_factor,
    gain,
    block_request_rows,
    adapter_of_block,
):
    rows, width = hidden.shape
    half_width = residual.shape[1]
    wide = lax.axis_size("wide")
    requests = wide * rows
    feature_count = output_weight.shape[0]
    adapters_here, rank, _ = adapter_down_factor.shape
    blocks = adapter_of_block.shape[0]
    swap = [(0, 1), (1, 0)]
    first, second = exchange_orders(wide)

    params = pltpu.CompilerParams(vmem_limit_bytes=16 * 2**20)

    def exchange(order, sent):
        return lax.all_to_all(sent, "wide", 0, 0, axis_index_groups=[order])

    sent = pl.pallas_call(
        functools.partial(pack, half_width),
        out_shape=jax.ShapeDtypeStruct((wide, rows, half_width), jnp.bfloat16),
        in_specs=[VMEM],
        out_specs=VMEM,
        compiler_params=params,
        name="pack",
    )(*in_hbm(hidden))
    half_rows = exchange(first, sent).reshape(requests, half_width)

    factor = (blocks, rank, half_width)
    weight, selected_down, selected_up, holds = pl.pallas_call(
        functools.partial(fetch, first, rows, adapters_here),
        out_shape=[pltpu.VMEM(output_weight.shape, jnp.bfloat16)]
        + [pltpu.VMEM(factor, jnp.bfloat16)] * 2
        + [pltpu.VMEM((requests, blocks * rank), jnp.float32)],
        in_specs=[SMEM, SMEM, HBM, HBM, HBM],
        out_specs=[VMEM] * 4,
        scratch_shapes=[pltpu.SemaphoreType.DMA((2 * blocks + 1,))],
        cost_estimate=pl.CostEstimate(
            flops=0, bytes_accessed=8 * blocks * rank * half_width, transcendentals=0
        ),
        compiler_params=params,
        name="fetch",
    )(
        *in_hbm(
            adapter_of_block,
            block_request_rows,
            output_weight,
            adapter_down_factor,
            adapter_up_factor,
        )
    )
    selected_down = selected_down.reshape(blocks * rank, half_width)
    selected_up = selected_up.reshape(blocks * rank, half_width)

    start = lax.axis_index("wide") * feature_count
    own_columns = lax.dynamic_slice_in_dim(half_rows, start % half_width, feature_count, 1)
    other_columns = lax.ppermute(own_columns, "tp", swap)
    inner_part = lax.dot_general(
        half_rows, selected_down, (((1,), (1,)), ((), ())), preferred_element_type=jnp.float32
    )
    inner_other = lax.ppermute(inner_part, "tp", swap)
    projected = pl.pallas_call(
        project,
        out_shape=pltpu.VMEM((requests, half_width), jnp.float32),
        in_specs=[VMEM] * 3,
        out_specs=VMEM,
        compiler_params=params,
        cost_estimate=pl.CostEstimate(
            flops=2 * requests * feature_count * half_width,
            bytes_accessed=2 * feature_count * half_width + 4 * requests * half_width,
            transcendentals=0,
        ),
        name="project",
    )(*in_vmem(own_columns, other_columns, weight))
    terms = pl.pallas_call(
        functools.partial(combine, first, second, rows),
        out_shape=pltpu.VMEM((wide, rows, half_width), jnp.bfloat16),
        in_specs=[VMEM] * 5,
        out_specs=VMEM,
        compiler_params=params,
        name="combine",
    )(*in_vmem(projected, inner_part, inner_other, holds, selected_up))
    terms = exchange(second, terms)
    summed = residual.astype(jnp.float32) + jnp.sum(terms.astype(jnp.float32), axis=0)
    squares = jnp.sum(summed * summed, axis=1, keepdims=True)
    squares += lax.ppermute(squares, "tp", swap)
    normed = summed * lax.rsqrt(squares / width + epsilon) * gain
    return (summed.astype(jnp.bfloat16), normed.astype(jnp.bfloat16))


def solution(mesh):
    return jax.shard_map(
        local,
        mesh=mesh,
        in_specs=(
            P(("grp", "wide"), None),
            P(("grp", "wide"), "tp"),
            P("wide", "tp"),
            P("wide", None, "tp"),
            P("wide", None, "tp"),
            P("tp"),
            P(("grp", "wide"), None),
            P(("grp", "wide")),
        ),
        out_specs=(P(("grp", "wide"), "tp"), P(("grp", "wide"), "tp")),
        check_vma=False,
    )
```

time: 28.8 us -> 27.7 us (0.962)
  waiting for transfers between devices: 5.27 us -> 3.49 us
  Pallas kernels: 3.5 us -> 4.68 us
  matrix products: 0.93 us -> 0.27 us
  starting transfers between devices: 7.95 us -> 8.5 us
  blocking collectives: 9.12 us -> 8.79 us
    all_to_all x1, waiting for transfers between devices: 3.47 us -> 2 us  [exchange(): return lax.all_to_all(sent, 'wide', 0, 0, axis_index_groups=[order])]
    pallas_call x2 -> x4, Pallas kernels: 3.5 us -> 4.68 us  [the longest x1 2.61 us: local(): pl.pallas_call(functools.partial(fetch, first, rows, adapters_here), out_...]
    dot_general x2 -> x0, matrix products: 0.67 us -> none  [the longest x1 0.46 us: local(): jnp.dot(own_features, output_weight, preferred_element_type=jnp.float32)]
    ppermute x1, waiting for transfers between devices: 0.7 us -> 0.04 us  [local(): inner_other = lax.ppermute(inner_part, 'tp', swap)]
    ppermute x1, starting transfers between devices: 0.07 us -> 0.55 us  [local(): inner_other = lax.ppermute(inner_part, 'tp', swap)]
    ppermute x0 -> x1, waiting for transfers between devices: none -> 0.35 us  [local(): other_columns = lax.ppermute(own_columns, 'tp', swap)]
    all_to_all x1, blocking collectives: 9.12 us -> 8.79 us  [exchange(): return lax.all_to_all(sent, 'wide', 0, 0, axis_index_groups=[order])]
  transfers between devices with their start and end apart: 3 -> 4, of which waited for: 3 -> 3; matrix products, arithmetic and copies ran while one was open for 2% -> 1% of each run, Pallas kernels for 7% -> 11%
where the time goes in v3:
time: 27.7 us; the launch traced here: 27.4 us
  blocking collectives  8.79 us (32%)
  starting transfers between devices  8.5 us (31%)
  Pallas kernels  4.68 us (17%)
  waiting for transfers between devices  3.49 us (13%)
  other arithmetic  0.89 us (3%)
  between operations  0.7 us (3%)
    all_to_all x1, blocking collectives, exchange(): return lax.all_to_all(sent, 'wide', 0, 0, axis_index_groups=[order])  8.79 us
    all_to_all x1, starting transfers between devices, exchange(): return lax.all_to_all(sent, 'wide', 0, 0, axis_index_groups=[order])  7.81 us
    pallas_call x1, Pallas kernels, local(): pl.pallas_call(functools.partial(fetch, first, rows, adapters_here), out_...  2.61 us
    all_to_all x1, waiting for transfers between devices, exchange(): return lax.all_to_all(sent, 'wide', 0, 0, axis_index_groups=[order])  2 us
    pallas_call x1, Pallas kernels, local(): pl.pallas_call(functools.partial(pack, half_width), out_shape=jax.ShapeDt...  1.41 us
    ppermute x1, waiting for transfers between devices, local(): squares += lax.ppermute(squares, 'tp', swap)  1.11 us
    convert_element_type x1, other arithmetic, local(): return (summed.astype(jnp.bfloat16), normed.astype(jnp.bfloat16))  0.69 us
  transfers between devices with their start and end apart: 4, of which 3 were waited for; matrix products, arithmetic and copies ran while one was open for 1% of the time, Pallas kernels for 11%

profile of v3, /device:TPU:0, one launch (start us, length us, event | category | flops | bytes accessed | tf_op | source)
XLA Modules:
  0.0 27.4 jit_solution(9815161072855906786)
XLA Ops:
  0.6 1.4 %pack.1 = bf16[8,4,2048]{2,1,0:T(4,128)(2,1)} custom-call(bf16[4,4096]{1,0:T(4,128)(2,1)} %hidden_ref.1), custom_call_target="tpu_custom_call" | custom-call | tf_op jit(solution)/shard_map/pack/pallas_call | solution.py:127
  2.0 7.8 %all-to-all-start = ((bf16[8,4,2048]{2,1,0:T(4,128)(2,1)}), bf16[8,4,2048]{2,1,0:T(4,128)(2,1)S(1)}, u32[]{:S(2)}, u32[]{:S(2)}) async-start(bf16[8,4,2048]{2,1,0:T(4,128)(2,1)} %pack.1), calls=%async_computation | async-start | bytes 262144 | tf_op jit(solution)/shard_map/all_to_all | solution.py:125
  9.9 2.6 %fetch.1 = (bf16[512,2048]{1,0:T(8,128)(2,1)S(1)}, bf16[2,64,2048]{2,1,0:T(8,128)(2,1)S(1)}, bf16[2,64,2048]{2,1,0:T(8,128)(2,1)S(1)}, f32[32,128]{1,0:T(8,128)S(1)}) custom-call(s32[2]{0:T(128)} %ids_ref.1, s32[2,4]{1,0:T(2,128)} %slots_ref.1, bf16[512,2048]{1,0:T(8,128)(2,1)} %weight_ref.1, bf16[8,64,2048]{2,1,0:T(8,128)(2,1)} %down_ref.1, ...), custom_call_target="tpu_custom_call" | custom-call | bytes 2097152 | tf_op jit(solution)/shard_map/fetch/pallas_call | solution.py:138
  12.5 2.0 %all-to-all-done = bf16[8,4,2048]{2,1,0:T(4,128)(2,1)S(1)} async-done(((bf16[8,4,2048]{2,1,0:T(4,128)(2,1)}), bf16[8,4,2048]{2,1,0:T(4,128)(2,1)S(1)}, u32[]{:S(2)}, u32[]{:S(2)}) %all-to-all-start) | async-done | bytes 131104 | tf_op jit(solution)/shard_map/all_to_all | solution.py:125
  14.5 0.1 collective-permute-start
  14.6 0.0 copy-start
  14.6 0.3 convolution_bitcast_fusion.own_ref
  14.9 0.0 copy-start.1
  14.9 0.6 %collective-permute-start.1 = (f32[32,128]{1,0:T(8,128)S(1)}, f32[32,128]{1,0:T(8,128)S(1)}, u32[]{:S(2)}, u32[]{:S(2)}) collective-permute-start(f32[32,128]{1,0:T(8,128)S(1)} %convolution_bitcast_fusion.own_ref), channel_id=1, source_target_pairs={{0,1},{1,0},{2,3},{3,2},{4,5},{5,4},{6,7},{7,6},{8,9},{9,8},{10,11... | collective-permute-start | bytes 49160 | tf_op jit(solution)/shard_map/ppermute | solution.py:169
  15.4 0.3 %collective-permute-done.other_columns_ref = bf16[32,512]{1,0:T(8,128)(2,1)S(1)} collective-permute-done((bf16[32,512]{1,0:T(8,128)(2,1)S(1)}, bf16[32,512]{1,0:T(8,128)(2,1)S(1)}, u32[]{:S(2)}, u32[]{:S(2)}) %collective-permute-start) | collective-permute-done | bytes 32800 | tf_op jit(solution)/shard_map/ppermute | solution.py:165
  15.8 0.5 %project.1.projected_ref = f32[32,2048]{1,0:T(8,128)S(1)} custom-call(bf16[32,512]{1,0:T(8,128)(2,1)S(1)} %constant_dynamic-slice_fusion.own_columns_ref, bf16[32,512]{1,0:T(8,128)(2,1)S(1)} %collective-permute-done.other_columns_ref, bf16[512,2048]{1,0:T(8,128)(2,1)S(1)} %get-tuple-element.6.weight_ref), custom_call_target="tpu_custom_call" | custom-call | flops 67108864 | bytes 2359296 | tf_op jit(solution)/shard_map/project/pallas_call | solution.py:170
  16.3 0.0 collective-permute-done.1.other_ref
  16.3 0.2 combine.1
  16.5 8.8 %all_to_all.10 = bf16[8,4,2048]{2,1,0:T(4,128)(2,1)S(1)} all-to-all(bf16[8,4,2048]{2,1,0:T(4,128)(2,1)S(1)} %combine.1), channel_id=1, replica_groups={{10,14,6,2,0,4,12,8},{11,15,7,3,1,5,13,9},{26,30,22,18,16,20,28,24},{27..., dimensions={0} | all-to-all | bytes 262144 | tf_op jit(solution)/shard_map/all_to_all | solution.py:125
  25.3 0.1 convert_reduce_fusion
  25.4 0.0 copy-done
  25.4 0.1 multiply_reduce_fusion
  25.5 0.1 collective-permute-start.2
  25.6 1.1 %collective-permute-done.2 = f32[4,1]{0,1:T(1,128)S(1)} collective-permute-done((f32[4,1]{0,1:T(1,128)S(1)}, f32[4,1]{0,1:T(1,128)S(1)}, u32[]{:S(2)}, u32[]{:S(2)}) %collective-permute-start.2) | collective-permute-done | bytes 48 | tf_op jit(solution)/shard_map/ppermute | solution.py:194
  26.7 0.0 copy-done.1
  26.7 0.7 %multiply_convert_fusion = (bf16[4,2048]{1,0:T(4,128)(2,1)}, bf16[4,2048]{1,0:T(4,128)(2,1)}) fusion(f32[2048]{0:T(1024)S(1)} %copy-done.1, f32[4]{0:T(128)S(1)} %rsqrt_bitcast_fusion, f32[4,2048]{1,0:T(4,128)S(1)} %convert_reduce_fusion, bf16[4,2048]{1,0:T(4,128)(2,1)S(1)} %copy-done), kind=kLoop, calls=%fused_computation.2 | loop fusion | flops 49152 | bytes 90128 | tf_op jit(solution)/shard_map/convert_element_type | solution.py:196
  (3 shorter events, 0.1 us)
Async XLA Ops:
  2.0 12.4 %all-to-all-start = ((bf16[8,4,2048]{2,1,0:T(4,128)(2,1)}), bf16[8,4,2048]{2,1,0:T(4,128)(2,1)S(1)}, u32[]{:S(2)}, u32[]{:S(2)}) async-start(bf16[8,4,2048]{2,1,0:T(4,128)(2,1)} %pack.1), calls=%async_computation | async-start | bytes 262144 | tf_op jit(solution)/shard_map/all_to_all | solution.py:125
  14.5 1.3 %collective-permute-start = (bf16[32,512]{1,0:T(8,128)(2,1)S(1)}, bf16[32,512]{1,0:T(8,128)(2,1)S(1)}, u32[]{:S(2)}, u32[]{:S(2)}) collective-permute-start(bf16[32,512]{1,0:T(8,128)(2,1)S(1)} %constant_dynamic-slice_fusion.own_columns_ref), channel_id=1, source_target_pairs={{0,1},{1,0},{2,3},{3,2},{4,5},{5,4},{6,7},{7,6},{8,9},{9,8},{10,11... | collective-permute-start | bytes 98312 | tf_op jit(solution)/shard_map/ppermute | solution.py:165
  14.6 10.8 %copy-start = (bf16[4,2048]{1,0:T(4,128)(2,1)S(1)}, bf16[4,2048]{1,0:T(4,128)(2,1)}, u32[]{:S(2)}) copy-start(bf16[4,2048]{1,0:T(4,128)(2,1)} %param.9) | copy-start | bytes 49156
  14.9 11.8 %copy-start.1 = (f32[2048]{0:T(1024)S(1)}, f32[2048]{0:T(1024)}, u32[]{:S(2)}) copy-start(f32[2048]{0:T(1024)} %param.13) | copy-start | bytes 24580
  14.9 1.4 %collective-permute-start.1 = (f32[32,128]{1,0:T(8,128)S(1)}, f32[32,128]{1,0:T(8,128)S(1)}, u32[]{:S(2)}, u32[]{:S(2)}) collective-permute-start(f32[32,128]{1,0:T(8,128)S(1)} %convolution_bitcast_fusion.own_ref), channel_id=1, source_target_pairs={{0,1},{1,0},{2,3},{3,2},{4,5},{5,4},{6,7},{7,6},{8,9},{9,8},{10,11... | collective-permute-start | bytes 49160 | tf_op jit(solution)/shard_map/ppermute | solution.py:169
  25.5 1.2 %collective-permute-start.2 = (f32[4,1]{0,1:T(1,128)S(1)}, f32[4,1]{0,1:T(1,128)S(1)}, u32[]{:S(2)}, u32[]{:S(2)}) collective-permute-start(f32[4,1]{0,1:T(1,128)S(1)} %bitcast.12), channel_id=1, source_target_pairs={{0,1},{1,0},{2,3},{3,2},{4,5},{5,4},{6,7},{7,6},{8,9},{9,8},{10,11... | collective-permute-start | bytes 56 | tf_op jit(solution)/shard_map/ppermute | solution.py:194

commit v4 on v3

--- a/solution.py
+++ b/solution.py
@@ -23,17 +23,26 @@
 
 def exchange_orders(wide):
     if wide == 8:
-        return [4, 1, 0, 3, 7, 2, 5, 6], [5, 7, 3, 1, 0, 2, 6, 4]
+        return [3, 2, 7, 0, 1, 6, 4, 5], [4, 6, 0, 7, 5, 1, 2, 3]
     middle = wide // 2
     order = [middle] + [index for index in range(wide) if index != middle]
     return order, order
 
 
-def pack(half_width, hidden_ref, sent_ref):
-    start = pl.multiple_of(lax.axis_index("tp") * half_width, 128)
-    half = hidden_ref[:, pl.ds(start, half_width)]
-    for place in range(sent_ref.shape[0]):
-        sent_ref[place] = half
+def core_in_first_group(device, wide):
+    return device // (wide // 2)
+
+
+def pack(order, half_width, hidden_ref, sent_ref):
+    wide = sent_ref.shape[0]
+    core = lax.axis_index("tp")
+    swapped = (core + core_in_first_group(lax.axis_index("wide"), wide)) % 2
+    halves = []
+    for member_core in range(2):
+        start = pl.multiple_of((member_core + swapped) % 2 * half_width, 128)
+        halves.append(hidden_ref[:, pl.ds(start, half_width)])
+    for place, device in enumerate(order):
+        sent_ref[place] = halves[core_in_first_group(device, wide)]
 
 
 def fetch(
@@ -121,18 +130,22 @@
 
     params = pltpu.CompilerParams(vmem_limit_bytes=16 * 2**20)
 
-    def exchange(order, sent):
-        return lax.all_to_all(sent, "wide", 0, 0, axis_index_groups=[order])
-
+    def exchange(sent, axes, groups):
+        return lax.all_to_all(sent, axes, 0, 0, axis_index_groups=groups)
+
+    groups = [
+        [2 * device + (core_in_first_group(device, wide) + group) % 2 for device in first]
+        for group in range(2)
+    ]
     sent = pl.pallas_call(
-        functools.partial(pack, half_width),
+        functools.partial(pack, first, half_width),
         out_shape=jax.ShapeDtypeStruct((wide, rows, half_width), jnp.bfloat16),
         in_specs=[VMEM],
         out_specs=VMEM,
         compiler_params=params,
         name="pack",
     )(*in_hbm(hidden))
-    half_rows = exchange(first, sent).reshape(requests, half_width)
+    half_rows = exchange(sent, ("wide", "tp"), groups).reshape(requests, half_width)
 
     factor = (blocks, rank, half_width)
     weight, selected_down, selected_up, holds = pl.pallas_call(
@@ -188,7 +201,7 @@
         compiler_params=params,
         name="combine",
     )(*in_vmem(projected, inner_part, inner_other, holds, selected_up))
-    terms = exchange(second, terms)
+    terms = exchange(terms, "wide", [second])
     summed = residual.astype(jnp.float32) + jnp.sum(terms.astype(jnp.float32), axis=0)
     squares = jnp.sum(summed * summed, axis=1, keepdims=True)
     squares += lax.ppermute(squares, "tp", swap)

time: 27.7 us -> 27.3 us (0.986)
  blocking collectives: 8.79 us -> 8.29 us
    ppermute x1, starting transfers between devices: 0.07 us -> 1.03 us  [local(): other_columns = lax.ppermute(own_columns, 'tp', swap)]
    all_to_all x1, starting transfers between devices: 7.81 us -> 7.25 us  [exchange(): return lax.all_to_all(sent, axes, 0, 0, axis_index_groups=groups)]
    all_to_all x1, blocking collectives: 8.79 us -> 8.29 us  [exchange(): return lax.all_to_all(sent, axes, 0, 0, axis_index_groups=groups)]
    ppermute x1, starting transfers between devices: 0.55 us -> 0.09 us  [local(): inner_other = lax.ppermute(inner_part, 'tp', swap)]
  transfers between devices with their start and end apart: 4 -> 4, of which waited for: 3 -> 4; matrix products, arithmetic and copies ran while one was open for 1% -> 1% of each run, Pallas kernels for 11% -> 11%
where the time goes in v4:
time: 27.3 us; the launch traced here: 27 us
  starting transfers between devices  8.43 us (31%)
  blocking collectives  8.29 us (30%)
  Pallas kernels  4.68 us (17%)
  waiting for transfers between devices  3.65 us (13%)
  other arithmetic  0.89 us (3%)
  between operations  0.69 us (3%)
    all_to_all x1, blocking collectives, exchange(): return lax.all_to_all(sent, axes, 0, 0, axis_index_groups=groups)  8.29 us
    all_to_all x1, starting transfers between devices, exchange(): return lax.all_to_all(sent, axes, 0, 0, axis_index_groups=groups)  7.25 us
    pallas_call x1, Pallas kernels, local(): pl.pallas_call(functools.partial(fetch, first, rows, adapters_here), out_...  2.61 us
    all_to_all x1, waiting for transfers between devices, exchange(): return lax.all_to_all(sent, axes, 0, 0, axis_index_groups=groups)  1.84 us
    pallas_call x1, Pallas kernels, local(): pl.pallas_call(functools.partial(pack, first, half_width), out_shape=jax....  1.41 us
    ppermute x1, waiting for transfers between devices, local(): squares += lax.ppermute(squares, 'tp', swap)  1.11 us
    ppermute x1, starting transfers between devices, local(): other_columns = lax.ppermute(own_columns, 'tp', swap)  1.03 us
    convert_element_type x1, other arithmetic, local(): return (summed.astype(jnp.bfloat16), normed.astype(jnp.bfloat16))  0.69 us
  transfers between devices with their start and end apart: 4, of which 4 were waited for; matrix products, arithmetic and copies ran while one was open for 1% of the time, Pallas kernels for 11%

profile of v4, /device:TPU:0, one launch (start us, length us, event | category | flops | bytes accessed | tf_op | source)
XLA Modules:
  0.0 27.0 jit_solution(15184623253099630317)
XLA Ops:
  0.6 1.4 %pack.1 = bf16[8,4,2048]{2,1,0:T(4,128)(2,1)} custom-call(bf16[4,4096]{1,0:T(4,128)(2,1)} %hidden_ref.1), custom_call_target="tpu_custom_call" | custom-call | tf_op jit(solution)/shard_map/pack/pallas_call | solution.py:140
  2.0 7.3 %all-to-all-start = ((bf16[8,4,2048]{2,1,0:T(4,128)(2,1)}), bf16[8,4,2048]{2,1,0:T(4,128)(2,1)S(1)}, u32[]{:S(2)}, u32[]{:S(2)}) async-start(bf16[8,4,2048]{2,1,0:T(4,128)(2,1)} %pack.1), calls=%async_computation | async-start | bytes 262144 | tf_op jit(solution)/shard_map/all_to_all | solution.py:134
  9.3 2.6 %fetch.1 = (bf16[512,2048]{1,0:T(8,128)(2,1)S(1)}, bf16[2,64,2048]{2,1,0:T(8,128)(2,1)S(1)}, bf16[2,64,2048]{2,1,0:T(8,128)(2,1)S(1)}, f32[32,128]{1,0:T(8,128)S(1)}) custom-call(s32[2]{0:T(128)} %ids_ref.1, s32[2,4]{1,0:T(2,128)} %slots_ref.1, bf16[512,2048]{1,0:T(8,128)(2,1)} %weight_ref.1, bf16[8,64,2048]{2,1,0:T(8,128)(2,1)} %down_ref.1, ...), custom_call_target="tpu_custom_call" | custom-call | bytes 2097152 | tf_op jit(solution)/shard_map/fetch/pallas_call | solution.py:151
  11.9 1.8 %all-to-all-done = bf16[8,4,2048]{2,1,0:T(4,128)(2,1)S(1)} async-done(((bf16[8,4,2048]{2,1,0:T(4,128)(2,1)}), bf16[8,4,2048]{2,1,0:T(4,128)(2,1)S(1)}, u32[]{:S(2)}, u32[]{:S(2)}) %all-to-all-start) | async-done | bytes 131104 | tf_op jit(solution)/shard_map/all_to_all | solution.py:134
  13.8 1.0 %collective-permute-start = (bf16[32,512]{1,0:T(8,128)(2,1)S(1)}, bf16[32,512]{1,0:T(8,128)(2,1)S(1)}, u32[]{:S(2)}, u32[]{:S(2)}) collective-permute-start(bf16[32,512]{1,0:T(8,128)(2,1)S(1)} %constant_dynamic-slice_fusion.own_columns_ref), channel_id=1, source_target_pairs={{0,1},{1,0},{2,3},{3,2},{4,5},{5,4},{6,7},{7,6},{8,9},{9,8},{10,11... | collective-permute-start | bytes 98312 | tf_op jit(solution)/shard_map/ppermute | solution.py:178
  14.8 0.0 copy-start
  14.8 0.3 convolution_bitcast_fusion.own_ref
  15.1 0.0 copy-start.1
  15.1 0.1 collective-permute-start.1
  15.2 0.5 %collective-permute-done.other_columns_ref = bf16[32,512]{1,0:T(8,128)(2,1)S(1)} collective-permute-done((bf16[32,512]{1,0:T(8,128)(2,1)S(1)}, bf16[32,512]{1,0:T(8,128)(2,1)S(1)}, u32[]{:S(2)}, u32[]{:S(2)}) %collective-permute-start) | collective-permute-done | bytes 32800 | tf_op jit(solution)/shard_map/ppermute | solution.py:178
  15.7 0.5 %project.1.projected_ref = f32[32,2048]{1,0:T(8,128)S(1)} custom-call(bf16[32,512]{1,0:T(8,128)(2,1)S(1)} %constant_dynamic-slice_fusion.own_columns_ref, bf16[32,512]{1,0:T(8,128)(2,1)S(1)} %collective-permute-done.other_columns_ref, bf16[512,2048]{1,0:T(8,128)(2,1)S(1)} %get-tuple-element.6.weight_ref), custom_call_target="tpu_custom_call" | custom-call | flops 67108864 | bytes 2359296 | tf_op jit(solution)/shard_map/project/pallas_call | solution.py:183
  16.1 0.2 collective-permute-done.1.other_ref
  16.4 0.2 combine.1
  16.6 8.3 %all_to_all.10 = bf16[8,4,2048]{2,1,0:T(4,128)(2,1)S(1)} all-to-all(bf16[8,4,2048]{2,1,0:T(4,128)(2,1)S(1)} %combine.1), channel_id=1, replica_groups={{8,12,0,14,10,2,4,6},{9,13,1,15,11,3,5,7},{24,28,16,30,26,18,20,22},{25..., dimensions={0} | all-to-all | bytes 262144 | tf_op jit(solution)/shard_map/all_to_all | solution.py:134
  24.9 0.1 convert_reduce_fusion
  24.9 0.0 copy-done
  24.9 0.1 multiply_reduce_fusion
  25.1 0.1 collective-permute-start.2
  25.1 1.1 %collective-permute-done.2 = f32[4,1]{0,1:T(1,128)S(1)} collective-permute-done((f32[4,1]{0,1:T(1,128)S(1)}, f32[4,1]{0,1:T(1,128)S(1)}, u32[]{:S(2)}, u32[]{:S(2)}) %collective-permute-start.2) | collective-permute-done | bytes 48 | tf_op jit(solution)/shard_map/ppermute | solution.py:207
  26.3 0.0 copy-done.1
  26.3 0.7 %multiply_convert_fusion = (bf16[4,2048]{1,0:T(4,128)(2,1)}, bf16[4,2048]{1,0:T(4,128)(2,1)}) fusion(f32[2048]{0:T(1024)S(1)} %copy-done.1, f32[4]{0:T(128)S(1)} %rsqrt_bitcast_fusion, f32[4,2048]{1,0:T(4,128)S(1)} %convert_reduce_fusion, bf16[4,2048]{1,0:T(4,128)(2,1)S(1)} %copy-done), kind=kLoop, calls=%fused_computation.2 | loop fusion | flops 49152 | bytes 90128 | tf_op jit(solution)/shard_map/convert_element_type | solution.py:209
  (3 shorter events, 0.1 us)
Async XLA Ops:
  2.0 11.7 %all-to-all-start = ((bf16[8,4,2048]{2,1,0:T(4,128)(2,1)}), bf16[8,4,2048]{2,1,0:T(4,128)(2,1)S(1)}, u32[]{:S(2)}, u32[]{:S(2)}) async-start(bf16[8,4,2048]{2,1,0:T(4,128)(2,1)} %pack.1), calls=%async_computation | async-start | bytes 262144 | tf_op jit(solution)/shard_map/all_to_all | solution.py:134
  13.8 1.9 %collective-permute-start = (bf16[32,512]{1,0:T(8,128)(2,1)S(1)}, bf16[32,512]{1,0:T(8,128)(2,1)S(1)}, u32[]{:S(2)}, u32[]{:S(2)}) collective-permute-start(bf16[32,512]{1,0:T(8,128)(2,1)S(1)} %constant_dynamic-slice_fusion.own_columns_ref), channel_id=1, source_target_pairs={{0,1},{1,0},{2,3},{3,2},{4,5},{5,4},{6,7},{7,6},{8,9},{9,8},{10,11... | collective-permute-start | bytes 98312 | tf_op jit(solution)/shard_map/ppermute | solution.py:178
  14.8 10.1 %copy-start = (bf16[4,2048]{1,0:T(4,128)(2,1)S(1)}, bf16[4,2048]{1,0:T(4,128)(2,1)}, u32[]{:S(2)}) copy-start(bf16[4,2048]{1,0:T(4,128)(2,1)} %param.9) | copy-start | bytes 49156
  15.1 11.2 %copy-start.1 = (f32[2048]{0:T(1024)S(1)}, f32[2048]{0:T(1024)}, u32[]{:S(2)}) copy-start(f32[2048]{0:T(1024)} %param.13) | copy-start | bytes 24580
  15.1 1.2 %collective-permute-start.1 = (f32[32,128]{1,0:T(8,128)S(1)}, f32[32,128]{1,0:T(8,128)S(1)}, u32[]{:S(2)}, u32[]{:S(2)}) collective-permute-start(f32[32,128]{1,0:T(8,128)S(1)} %convolution_bitcast_fusion.own_ref), channel_id=1, source_target_pairs={{0,1},{1,0},{2,3},{3,2},{4,5},{5,4},{6,7},{7,6},{8,9},{9,8},{10,11... | collective-permute-start | bytes 49160 | tf_op jit(solution)/shard_map/ppermute | solution.py:182
  25.1 1.2 %collective-permute-start.2 = (f32[4,1]{0,1:T(1,128)S(1)}, f32[4,1]{0,1:T(1,128)S(1)}, u32[]{:S(2)}, u32[]{:S(2)}) collective-permute-start(f32[4,1]{0,1:T(1,128)S(1)} %bitcast.12), channel_id=1, source_target_pairs={{0,1},{1,0},{2,3},{3,2},{4,5},{5,4},{6,7},{7,6},{8,9},{9,8},{10,11... | collective-permute-start | bytes 56 | tf_op jit(solution)/shard_map/ppermute | solution.py:207

commit v5 on v4

--- a/solution.py
+++ b/solution.py
@@ -23,7 +23,7 @@
 
 def exchange_orders(wide):
     if wide == 8:
-        return [3, 2, 7, 0, 1, 6, 4, 5], [4, 6, 0, 7, 5, 1, 2, 3]
+        return [3, 4, 7, 0, 1, 6, 2, 5], [4, 6, 0, 7, 5, 1, 2, 3]
     middle = wide // 2
     order = [middle] + [index for index in range(wide) if index != middle]
     return order, order
@@ -58,15 +58,16 @@
     down_out,
     up_out,
     holds_out,
+    down_rows,
     sems,
 ):
-    blocks, rank, _ = down_out.shape
+    blocks, rank, _ = up_out.shape
     base = lax.axis_index("wide") * adapters_here
     copies = [pltpu.make_async_copy(weight_ref, weight_out, sems.at[2 * blocks])]
     for block in range(blocks):
         adapter = jnp.clip(ids_ref[block] - base, 0, adapters_here - 1)
         copies.append(
-            pltpu.make_async_copy(down_ref.at[adapter], down_out.at[block], sems.at[2 * block])
+            pltpu.make_async_copy(down_ref.at[adapter], down_rows.at[block], sems.at[2 * block])
         )
         copies.append(
             pltpu.make_async_copy(up_ref.at[adapter], up_out.at[block], sems.at[2 * block + 1])
@@ -88,6 +89,8 @@
         holds_out[:, block * rank : (block + 1) * rank] = held.astype(jnp.float32)
     for copy in copies:
         copy.wait()
+    for block in range(blocks):
+        down_out[:, block * rank : (block + 1) * rank] = down_rows[block].T
 
 
 def project(own_columns_ref, other_columns_ref, weight_ref, projected_ref):
@@ -151,11 +154,14 @@
     weight, selected_down, selected_up, holds = pl.pallas_call(
         functools.partial(fetch, first, rows, adapters_here),
         out_shape=[pltpu.VMEM(output_weight.shape, jnp.bfloat16)]
-        + [pltpu.VMEM(factor, jnp.bfloat16)] * 2
+        + [pltpu.VMEM((half_width, blocks * rank), jnp.bfloat16), pltpu.VMEM(factor, jnp.bfloat16)]
         + [pltpu.VMEM((requests, blocks * rank), jnp.float32)],
         in_specs=[SMEM, SMEM, HBM, HBM, HBM],
         out_specs=[VMEM] * 4,
-        scratch_shapes=[pltpu.SemaphoreType.DMA((2 * blocks + 1,))],
+        scratch_shapes=[
+            pltpu.VMEM(factor, jnp.bfloat16),
+            pltpu.SemaphoreType.DMA((2 * blocks + 1,)),
+        ],
         cost_estimate=pl.CostEstimate(
             flops=0, bytes_accessed=8 * blocks * rank * half_width, transcendentals=0
         ),
@@ -170,15 +176,12 @@
             adapter_up_factor,
         )
     )
-    selected_down = selected_down.reshape(blocks * rank, half_width)
     selected_up = selected_up.reshape(blocks * rank, half_width)
 
     start = lax.axis_index("wide") * feature_count
     own_columns = lax.dynamic_slice_in_dim(half_rows, start % half_width, feature_count, 1)
     other_columns = lax.ppermute(own_columns, "tp", swap)
-    inner_part = lax.dot_general(
-        half_rows, selected_down, (((1,), (1,)), ((), ())), preferred_element_type=jnp.float32
-    )
+    inner_part = jnp.dot(half_rows, selected_down, preferred_element_type=jnp.float32)
     inner_other = lax.ppermute(inner_part, "tp", swap)
     projected = pl.pallas_call(
         project,

time: 27.3 us -> 27.2 us (level)
  Pallas kernels: 4.68 us -> 5.31 us
  waiting for transfers between devices: 3.65 us -> 3.02 us
    all_to_all x1, waiting for transfers between devices: 1.84 us -> 1.21 us  [exchange(): return lax.all_to_all(sent, axes, 0, 0, axis_index_groups=groups)]
    pallas_call x1, Pallas kernels: 2.61 us -> 3.24 us  [local(): pl.pallas_call(functools.partial(fetch, first, rows, adapters_here), out_...]
  transfers between devices with their start and end apart: 4 -> 4, of which waited for: 4 -> 4; matrix products, arithmetic and copies ran while one was open for 1% -> 1% of each run, Pallas kernels for 11% -> 14%
where the time goes in v5:
time: 27.2 us; the launch traced here: 26.9 us
  blocking collectives  8.45 us (31%)
  starting transfers between devices  8.3 us (31%)
  Pallas kernels  5.31 us (20%)
  waiting for transfers between devices  3.02 us (11%)
  other arithmetic  0.89 us (3%)
  between operations  0.69 us (3%)
    all_to_all x1, blocking collectives, exchange(): return lax.all_to_all(sent, axes, 0, 0, axis_index_groups=groups)  8.45 us
    all_to_all x1, starting transfers between devices, exchange(): return lax.all_to_all(sent, axes, 0, 0, axis_index_groups=groups)  7.25 us
    pallas_call x1, Pallas kernels, local(): pl.pallas_call(functools.partial(fetch, first, rows, adapters_here), out_...  3.24 us
    pallas_call x1, Pallas kernels, local(): pl.pallas_call(functools.partial(pack, first, half_width), out_shape=jax....  1.41 us
    all_to_all x1, waiting for transfers between devices, exchange(): return lax.all_to_all(sent, axes, 0, 0, axis_index_groups=groups)  1.21 us
    ppermute x1, waiting for transfers between devices, local(): squares += lax.ppermute(squares, 'tp', swap)  1.11 us
    ppermute x1, starting transfers between devices, local(): other_columns = lax.ppermute(own_columns, 'tp', swap)  0.89 us
    convert_element_type x1, other arithmetic, local(): return (summed.astype(jnp.bfloat16), normed.astype(jnp.bfloat16))  0.69 us
  transfers between devices with their start and end apart: 4, of which 4 were waited for; matrix products, arithmetic and copies ran while one was open for 1% of the time, Pallas kernels for 14%

profile of v5, /device:TPU:0, one launch (start us, length us, event | category | flops | bytes accessed | tf_op | source)
XLA Modules:
  0.0 26.9 jit_solution(9820983476371654331)
XLA Ops:
  0.6 1.4 %pack.1 = bf16[8,4,2048]{2,1,0:T(4,128)(2,1)} custom-call(bf16[4,4096]{1,0:T(4,128)(2,1)} %hidden_ref.1), custom_call_target="tpu_custom_call" | custom-call | tf_op jit(solution)/shard_map/pack/pallas_call | solution.py:143
  2.0 7.3 %all-to-all-start = ((bf16[8,4,2048]{2,1,0:T(4,128)(2,1)}), bf16[8,4,2048]{2,1,0:T(4,128)(2,1)S(1)}, u32[]{:S(2)}, u32[]{:S(2)}) async-start(bf16[8,4,2048]{2,1,0:T(4,128)(2,1)} %pack.1), calls=%async_computation | async-start | bytes 262144 | tf_op jit(solution)/shard_map/all_to_all | solution.py:137
  9.3 3.2 %fetch.1 = (bf16[512,2048]{1,0:T(8,128)(2,1)S(1)}, bf16[2048,128]{1,0:T(8,128)(2,1)S(1)}, bf16[2,64,2048]{2,1,0:T(8,128)(2,1)S(1)}, f32[32,128]{1,0:T(8,128)S(1)}) custom-call(s32[2]{0:T(128)} %ids_ref.1, s32[2,4]{1,0:T(2,128)} %slots_ref.1, bf16[512,2048]{1,0:T(8,128)(2,1)} %weight_ref.1, bf16[8,64,2048]{2,1,0:T(8,128)(2,1)} %down_ref.1, ...), custom_call_target="tpu_custom_call" | custom-call | bytes 2097152 | tf_op jit(solution)/shard_map/fetch/pallas_call | solution.py:154
  12.5 1.2 %all-to-all-done = bf16[8,4,2048]{2,1,0:T(4,128)(2,1)S(1)} async-done(((bf16[8,4,2048]{2,1,0:T(4,128)(2,1)}), bf16[8,4,2048]{2,1,0:T(4,128)(2,1)S(1)}, u32[]{:S(2)}, u32[]{:S(2)}) %all-to-all-start) | async-done | bytes 131104 | tf_op jit(solution)/shard_map/all_to_all | solution.py:137
  13.8 0.9 %collective-permute-start = (bf16[32,512]{1,0:T(8,128)(2,1)S(1)}, bf16[32,512]{1,0:T(8,128)(2,1)S(1)}, u32[]{:S(2)}, u32[]{:S(2)}) collective-permute-start(bf16[32,512]{1,0:T(8,128)(2,1)S(1)} %constant_dynamic-slice_fusion.own_columns_ref), channel_id=1, source_target_pairs={{0,1},{1,0},{2,3},{3,2},{4,5},{5,4},{6,7},{7,6},{8,9},{9,8},{10,11... | collective-permute-start | bytes 98312 | tf_op jit(solution)/shard_map/ppermute | solution.py:183
  14.7 0.0 copy-start
  14.7 0.2 convolution_bitcast_fusion.own_ref
  14.9 0.0 copy-start.1
  14.9 0.1 collective-permute-start.1
  15.0 0.6 %collective-permute-done.other_columns_ref = bf16[32,512]{1,0:T(8,128)(2,1)S(1)} collective-permute-done((bf16[32,512]{1,0:T(8,128)(2,1)S(1)}, bf16[32,512]{1,0:T(8,128)(2,1)S(1)}, u32[]{:S(2)}, u32[]{:S(2)}) %collective-permute-start) | collective-permute-done | bytes 32800 | tf_op jit(solution)/shard_map/ppermute | solution.py:183
  15.6 0.5 %project.1.projected_ref = f32[32,2048]{1,0:T(8,128)S(1)} custom-call(bf16[32,512]{1,0:T(8,128)(2,1)S(1)} %constant_dynamic-slice_fusion.own_columns_ref, bf16[32,512]{1,0:T(8,128)(2,1)S(1)} %collective-permute-done.other_columns_ref, bf16[512,2048]{1,0:T(8,128)(2,1)S(1)} %get-tuple-element.6.weight_ref), custom_call_target="tpu_custom_call" | custom-call | flops 67108864 | bytes 2359296 | tf_op jit(solution)/shard_map/project/pallas_call | solution.py:186
  16.0 0.1 collective-permute-done.1.other_ref
  16.2 0.2 combine.1
  16.4 8.4 %all_to_all.10 = bf16[8,4,2048]{2,1,0:T(4,128)(2,1)S(1)} all-to-all(bf16[8,4,2048]{2,1,0:T(4,128)(2,1)S(1)} %combine.1), channel_id=1, replica_groups={{8,12,0,14,10,2,4,6},{9,13,1,15,11,3,5,7},{24,28,16,30,26,18,20,22},{25..., dimensions={0} | all-to-all | bytes 262144 | tf_op jit(solution)/shard_map/all_to_all | solution.py:137
  24.8 0.1 convert_reduce_fusion
  24.9 0.0 copy-done
  24.9 0.1 multiply_reduce_fusion
  25.0 0.1 collective-permute-start.2
  25.1 1.1 %collective-permute-done.2 = f32[4,1]{0,1:T(1,128)S(1)} collective-permute-done((f32[4,1]{0,1:T(1,128)S(1)}, f32[4,1]{0,1:T(1,128)S(1)}, u32[]{:S(2)}, u32[]{:S(2)}) %collective-permute-start.2) | collective-permute-done | bytes 48 | tf_op jit(solution)/shard_map/ppermute | solution.py:210
  26.2 0.0 copy-done.1
  26.2 0.7 %multiply_convert_fusion = (bf16[4,2048]{1,0:T(4,128)(2,1)}, bf16[4,2048]{1,0:T(4,128)(2,1)}) fusion(f32[2048]{0:T(1024)S(1)} %copy-done.1, f32[4]{0:T(128)S(1)} %rsqrt_bitcast_fusion, f32[4,2048]{1,0:T(4,128)S(1)} %convert_reduce_fusion, bf16[4,2048]{1,0:T(4,128)(2,1)S(1)} %copy-done), kind=kLoop, calls=%fused_computation.2 | loop fusion | flops 49152 | bytes 90128 | tf_op jit(solution)/shard_map/convert_element_type | solution.py:212
  (3 shorter events, 0.1 us)
Async XLA Ops:
  2.0 11.7 %all-to-all-start = ((bf16[8,4,2048]{2,1,0:T(4,128)(2,1)}), bf16[8,4,2048]{2,1,0:T(4,128)(2,1)S(1)}, u32[]{:S(2)}, u32[]{:S(2)}) async-start(bf16[8,4,2048]{2,1,0:T(4,128)(2,1)} %pack.1), calls=%async_computation | async-start | bytes 262144 | tf_op jit(solution)/shard_map/all_to_all | solution.py:137
  13.8 1.8 %collective-permute-start = (bf16[32,512]{1,0:T(8,128)(2,1)S(1)}, bf16[32,512]{1,0:T(8,128)(2,1)S(1)}, u32[]{:S(2)}, u32[]{:S(2)}) collective-permute-start(bf16[32,512]{1,0:T(8,128)(2,1)S(1)} %constant_dynamic-slice_fusion.own_columns_ref), channel_id=1, source_target_pairs={{0,1},{1,0},{2,3},{3,2},{4,5},{5,4},{6,7},{7,6},{8,9},{9,8},{10,11... | collective-permute-start | bytes 98312 | tf_op jit(solution)/shard_map/ppermute | solution.py:183
  14.7 10.2 %copy-start = (bf16[4,2048]{1,0:T(4,128)(2,1)S(1)}, bf16[4,2048]{1,0:T(4,128)(2,1)}, u32[]{:S(2)}) copy-start(bf16[4,2048]{1,0:T(4,128)(2,1)} %param.9) | copy-start | bytes 49156
  14.9 11.3 %copy-start.1 = (f32[2048]{0:T(1024)S(1)}, f32[2048]{0:T(1024)}, u32[]{:S(2)}) copy-start(f32[2048]{0:T(1024)} %param.13) | copy-start | bytes 24580
  14.9 1.2 %collective-permute-start.1 = (f32[32,128]{1,0:T(8,128)S(1)}, f32[32,128]{1,0:T(8,128)S(1)}, u32[]{:S(2)}, u32[]{:S(2)}) collective-permute-start(f32[32,128]{1,0:T(8,128)S(1)} %convolution_bitcast_fusion.own_ref), channel_id=1, source_target_pairs={{0,1},{1,0},{2,3},{3,2},{4,5},{5,4},{6,7},{7,6},{8,9},{9,8},{10,11... | collective-permute-start | bytes 49160 | tf_op jit(solution)/shard_map/ppermute | solution.py:185
  25.0 1.2 %collective-permute-start.2 = (f32[4,1]{0,1:T(1,128)S(1)}, f32[4,1]{0,1:T(1,128)S(1)}, u32[]{:S(2)}, u32[]{:S(2)}) collective-permute-start(f32[4,1]{0,1:T(1,128)S(1)} %bitcast.10), channel_id=1, source_target_pairs={{0,1},{1,0},{2,3},{3,2},{4,5},{5,4},{6,7},{7,6},{8,9},{9,8},{10,11... | collective-permute-start | bytes 56 | tf_op jit(solution)/shard_map/ppermute | solution.py:210

commit v6 on v4

--- a/solution.py
+++ b/solution.py
@@ -54,10 +54,12 @@
     weight_ref,
     down_ref,
     up_ref,
+    residual_ref,
     weight_out,
     down_out,
     up_out,
     holds_out,
+    residual_out,
     sems,
 ):
     blocks, rank, _ = down_out.shape
@@ -73,6 +75,7 @@
         )
     for copy in copies:
         copy.start()
+    residual_out[...] = residual_ref[...].astype(jnp.float32)
     requests = holds_out.shape[0]
     line = lax.broadcasted_iota(jnp.int32, (requests, rank), 0)
     place, within = line // rows, line % rows
@@ -106,6 +109,15 @@
     for place, device in enumerate(second):
         start = first.index(device) * rows
         sent_ref[place] = total[start : start + rows].astype(sent_ref.dtype)
+
+
+def home(terms_ref, residual_ref, summed_ref, squares_ref):
+    summed = residual_ref[...]
+    for place in range(terms_ref.shape[0]):
+        summed += terms_ref[place].astype(jnp.float32)
+    summed_ref[...] = summed
+    squares = jnp.sum(summed * summed, axis=1, keepdims=True)
+    squares_ref[...] = squares
 
 
 def local(
@@ -148,13 +160,16 @@
     half_rows = exchange(sent, ("wide", "tp"), groups).reshape(requests, half_width)
 
     factor = (blocks, rank, half_width)
-    weight, selected_down, selected_up, holds = pl.pallas_call(
+    weight, selected_down, selected_up, holds, residual_here = pl.pallas_call(
         functools.partial(fetch, first, rows, adapters_here),
         out_shape=[pltpu.VMEM(output_weight.shape, jnp.bfloat16)]
         + [pltpu.VMEM(factor, jnp.bfloat16)] * 2
-        + [pltpu.VMEM((requests, blocks * rank), jnp.float32)],
-        in_specs=[SMEM, SMEM, HBM, HBM, HBM],
-        out_specs=[VMEM] * 4,
+        + [
+            pltpu.VMEM((requests, blocks * rank), jnp.float32),
+            pltpu.VMEM((rows, half_width), jnp.float32),
+        ],
+        in_specs=[SMEM, SMEM, HBM, HBM, HBM, VMEM],
+        out_specs=[VMEM] * 5,
         scratch_shapes=[pltpu.SemaphoreType.DMA((2 * blocks + 1,))],
         cost_estimate=pl.CostEstimate(
             flops=0, bytes_accessed=8 * blocks * rank * half_width, transcendentals=0
@@ -168,6 +183,7 @@
             output_weight,
             adapter_down_factor,
             adapter_up_factor,
+            residual,
         )
     )
     selected_down = selected_down.reshape(blocks * rank, half_width)
@@ -202,8 +218,17 @@
         name="combine",
     )(*in_vmem(projected, inner_part, inner_other, holds, selected_up))
     terms = exchange(terms, "wide", [second])
-    summed = residual.astype(jnp.float32) + jnp.sum(terms.astype(jnp.float32), axis=0)
-    squares = jnp.sum(summed * summed, axis=1, keepdims=True)
+    summed, squares = pl.pallas_call(
+        home,
+        out_shape=[
+            pltpu.VMEM((rows, half_width), jnp.float32),
+            pltpu.VMEM((rows, 1), jnp.float32),
+        ],
+        in_specs=[VMEM] * 2,
+        out_specs=[VMEM] * 2,
+        compiler_params=params,
+        name="home",
+    )(*in_vmem(terms, residual_here))
     squares += lax.ppermute(squares, "tp", swap)
     normed = summed * lax.rsqrt(squares / width + epsilon) * gain
     return (summed.astype(jnp.bfloat16), normed.astype(jnp.bfloat16))

time: 27.3 us -> 27.3 us (level)
  no operation moved by 1% of the time
where the time goes in v6:
time: 27.3 us; the launch traced here: 26.9 us
  starting transfers between devices  8.33 us (31%)
  blocking collectives  8.3 us (30%)
  Pallas kernels  4.77 us (17%)
  waiting for transfers between devices  3.72 us (14%)
  other arithmetic  0.8 us (3%)
  between operations  0.67 us (2%)
    all_to_all x1, blocking collectives, exchange(): return lax.all_to_all(sent, axes, 0, 0, axis_index_groups=groups)  8.3 us
    all_to_all x1, starting transfers between devices, exchange(): return lax.all_to_all(sent, axes, 0, 0, axis_index_groups=groups)  7.25 us
    pallas_call x1, Pallas kernels, local(): pl.pallas_call(functools.partial(fetch, first, rows, adapters_here), out_...  2.59 us
    all_to_all x1, waiting for transfers between devices, exchange(): return lax.all_to_all(sent, axes, 0, 0, axis_index_groups=groups)  1.86 us
    pallas_call x1, Pallas kernels, local(): pl.pallas_call(functools.partial(pack, first, half_width), out_shape=jax....  1.42 us
    ppermute x1, waiting for transfers between devices, local(): squares += lax.ppermute(squares, 'tp', swap)  1.15 us
    ppermute x1, starting transfers between devices, local(): other_columns = lax.ppermute(own_columns, 'tp', swap)  1.03 us
    convert_element_type x1, other arithmetic, local(): return (summed.astype(jnp.bfloat16), normed.astype(jnp.bfloat16))  0.69 us
  transfers between devices with their start and end apart: 4, of which 4 were waited for; matrix products, arithmetic and copies ran while one was open for 1% of the time, Pallas kernels for 11%

profile of v6, /device:TPU:0, one launch (start us, length us, event | category | flops | bytes accessed | tf_op | source)
XLA Modules:
  0.0 26.9 jit_solution(12870610021594400295)
XLA Ops:
  0.6 1.4 %pack.1 = bf16[8,4,2048]{2,1,0:T(4,128)(2,1)} custom-call(bf16[4,4096]{1,0:T(4,128)(2,1)} %hidden_ref.1), custom_call_target="tpu_custom_call" | custom-call | tf_op jit(solution)/shard_map/pack/pallas_call | solution.py:152
  2.0 7.3 %all-to-all-start = ((bf16[8,4,2048]{2,1,0:T(4,128)(2,1)}), bf16[8,4,2048]{2,1,0:T(4,128)(2,1)S(1)}, u32[]{:S(2)}, u32[]{:S(2)}) async-start(bf16[8,4,2048]{2,1,0:T(4,128)(2,1)} %pack.1), calls=%async_computation | async-start | bytes 262144 | tf_op jit(solution)/shard_map/all_to_all | solution.py:146
  9.3 2.6 %fetch.1 = (bf16[512,2048]{1,0:T(8,128)(2,1)S(1)}, bf16[2,64,2048]{2,1,0:T(8,128)(2,1)S(1)}, bf16[2,64,2048]{2,1,0:T(8,128)(2,1)S(1)}, f32[32,128]{1,0:T(8,128)S(1)}, f32[4,2048]{1,0:T(4,128)S(1)}) custom-call(s32[2]{0:T(128)} %ids_ref.1, s32[2,4]{1,0:T(2,128)} %slots_ref.1, bf16[512,2048]{1,0:T(8,128)(2,1)} %weight_ref.1, bf16[8,64,2048]{2,1,0:T(8,128)(2,1)} %down_ref.1, ...), custom_call_target="tpu_custom_call" | custom-call | bytes 2097152 | tf_op jit(solution)/shard_map/fetch/pallas_call | solution.py:163
  11.9 1.9 %all-to-all-done = bf16[8,4,2048]{2,1,0:T(4,128)(2,1)S(1)} async-done(((bf16[8,4,2048]{2,1,0:T(4,128)(2,1)}), bf16[8,4,2048]{2,1,0:T(4,128)(2,1)S(1)}, u32[]{:S(2)}, u32[]{:S(2)}) %all-to-all-start) | async-done | bytes 131104 | tf_op jit(solution)/shard_map/all_to_all | solution.py:146
  13.8 1.0 %collective-permute-start = (bf16[32,512]{1,0:T(8,128)(2,1)S(1)}, bf16[32,512]{1,0:T(8,128)(2,1)S(1)}, u32[]{:S(2)}, u32[]{:S(2)}) collective-permute-start(bf16[32,512]{1,0:T(8,128)(2,1)S(1)} %constant_dynamic-slice_fusion.own_columns_ref), channel_id=1, source_target_pairs={{0,1},{1,0},{2,3},{3,2},{4,5},{5,4},{6,7},{7,6},{8,9},{9,8},{10,11... | collective-permute-start | bytes 98312 | tf_op jit(solution)/shard_map/ppermute | solution.py:194
  14.8 0.0 copy-start
  14.8 0.3 convolution_bitcast_fusion.own_ref
  15.1 0.0 collective-permute-start.1
  15.2 0.5 %collective-permute-done.other_columns_ref = bf16[32,512]{1,0:T(8,128)(2,1)S(1)} collective-permute-done((bf16[32,512]{1,0:T(8,128)(2,1)S(1)}, bf16[32,512]{1,0:T(8,128)(2,1)S(1)}, u32[]{:S(2)}, u32[]{:S(2)}) %collective-permute-start) | collective-permute-done | bytes 32800 | tf_op jit(solution)/shard_map/ppermute | solution.py:194
  15.7 0.5 %project.1.projected_ref = f32[32,2048]{1,0:T(8,128)S(1)} custom-call(bf16[32,512]{1,0:T(8,128)(2,1)S(1)} %constant_dynamic-slice_fusion.own_columns_ref, bf16[32,512]{1,0:T(8,128)(2,1)S(1)} %collective-permute-done.other_columns_ref, bf16[512,2048]{1,0:T(8,128)(2,1)S(1)} %get-tuple-element.9.weight_ref), custom_call_target="tpu_custom_call" | custom-call | flops 67108864 | bytes 2359296 | tf_op jit(solution)/shard_map/project/pallas_call | solution.py:199
  16.1 0.2 collective-permute-done.1.other_ref
  16.3 0.2 combine.1
  16.5 8.3 %all_to_all.10.terms_ref = bf16[8,4,2048]{2,1,0:T(4,128)(2,1)S(1)} all-to-all(bf16[8,4,2048]{2,1,0:T(4,128)(2,1)S(1)} %combine.1), channel_id=1, replica_groups={{8,12,0,14,10,2,4,6},{9,13,1,15,11,3,5,7},{24,28,16,30,26,18,20,22},{25..., dimensions={0} | all-to-all | bytes 262144 | tf_op jit(solution)/shard_map/all_to_all | solution.py:146
  24.8 0.1 home.1
  24.9 0.0 collective-permute-start.2
  24.9 1.2 %collective-permute-done.2 = f32[4,1]{1,0:T(4,128)S(1)} collective-permute-done((f32[4,1]{1,0:T(4,128)S(1)}, f32[4,1]{1,0:T(4,128)S(1)}, u32[]{:S(2)}, u32[]{:S(2)}) %collective-permute-start.2) | collective-permute-done | bytes 48 | tf_op jit(solution)/shard_map/ppermute | solution.py:232
  26.1 0.1 rsqrt_reduce_fusion
  26.2 0.0 copy-done
  26.2 0.7 %multiply_convert_fusion = (bf16[4,2048]{1,0:T(4,128)(2,1)}, bf16[4,2048]{1,0:T(4,128)(2,1)}) fusion(f32[4,2048]{1,0:T(4,128)S(1)} %get-tuple-element.14, f32[2048]{0:T(1024)S(1)} %copy-done, f32[4]{0:T(128)S(1)} %rsqrt_reduce_fusion), kind=kLoop, calls=%fused_computation.1 | loop fusion | flops 32768 | bytes 73744 | tf_op jit(solution)/shard_map/convert_element_type | solution.py:234
  (2 shorter events, 0.0 us)
Async XLA Ops:
  2.0 11.7 %all-to-all-start = ((bf16[8,4,2048]{2,1,0:T(4,128)(2,1)}), bf16[8,4,2048]{2,1,0:T(4,128)(2,1)S(1)}, u32[]{:S(2)}, u32[]{:S(2)}) async-start(bf16[8,4,2048]{2,1,0:T(4,128)(2,1)} %pack.1), calls=%async_computation | async-start | bytes 262144 | tf_op jit(solution)/shard_map/all_to_all | solution.py:146
  13.8 1.9 %collective-permute-start = (bf16[32,512]{1,0:T(8,128)(2,1)S(1)}, bf16[32,512]{1,0:T(8,128)(2,1)S(1)}, u32[]{:S(2)}, u32[]{:S(2)}) collective-permute-start(bf16[32,512]{1,0:T(8,128)(2,1)S(1)} %constant_dynamic-slice_fusion.own_columns_ref), channel_id=1, source_target_pairs={{0,1},{1,0},{2,3},{3,2},{4,5},{5,4},{6,7},{7,6},{8,9},{9,8},{10,11... | collective-permute-start | bytes 98312 | tf_op jit(solution)/shard_map/ppermute | solution.py:194
  14.8 11.4 %copy-start = (f32[2048]{0:T(1024)S(1)}, f32[2048]{0:T(1024)}, u32[]{:S(2)}) copy-start(f32[2048]{0:T(1024)} %param.13) | copy-start | bytes 24580
  15.1 1.2 %collective-permute-start.1 = (f32[32,128]{1,0:T(8,128)S(1)}, f32[32,128]{1,0:T(8,128)S(1)}, u32[]{:S(2)}, u32[]{:S(2)}) collective-permute-start(f32[32,128]{1,0:T(8,128)S(1)} %convolution_bitcast_fusion.own_ref), channel_id=1, source_target_pairs={{0,1},{1,0},{2,3},{3,2},{4,5},{5,4},{6,7},{7,6},{8,9},{9,8},{10,11... | collective-permute-start | bytes 49160 | tf_op jit(solution)/shard_map/ppermute | solution.py:198
  24.9 1.2 %collective-permute-start.2 = (f32[4,1]{1,0:T(4,128)S(1)}, f32[4,1]{1,0:T(4,128)S(1)}, u32[]{:S(2)}, u32[]{:S(2)}) collective-permute-start(f32[4,1]{1,0:T(4,128)S(1)} %get-tuple-element.15), channel_id=1, source_target_pairs={{0,1},{1,0},{2,3},{3,2},{4,5},{5,4},{6,7},{7,6},{8,9},{9,8},{10,11... | collective-permute-start | bytes 56 | tf_op jit(solution)/shard_map/ppermute | solution.py:232

commit v7 on v4

--- a/solution.py
+++ b/solution.py
@@ -145,7 +145,8 @@
         compiler_params=params,
         name="pack",
     )(*in_hbm(hidden))
-    half_rows = exchange(sent, ("wide", "tp"), groups).reshape(requests, half_width)
+    received = exchange(sent, ("wide", "tp"), groups)
+    half_rows = received.reshape(requests, half_width)
 
     factor = (blocks, rank, half_width)
     weight, selected_down, selected_up, holds = pl.pallas_call(
@@ -174,8 +175,9 @@
     selected_up = selected_up.reshape(blocks * rank, half_width)
 
     start = lax.axis_index("wide") * feature_count
-    own_columns = lax.dynamic_slice_in_dim(half_rows, start % half_width, feature_count, 1)
-    other_columns = lax.ppermute(own_columns, "tp", swap)
+    own_columns = lax.dynamic_slice_in_dim(received, start % half_width, feature_count, 2)
+    other_columns = lax.ppermute(own_columns, "tp", swap).reshape(requests, feature_count)
+    own_columns = own_columns.reshape(requests, feature_count)
     inner_part = lax.dot_general(
         half_rows, selected_down, (((1,), (1,)), ((), ())), preferred_element_type=jnp.float32
     )

time: 27.3 us -> 27.3 us (level)
  no operation moved by 1% of the time
where the time goes in v7:
time: 27.3 us; the launch traced here: 27 us
  starting transfers between devices  8.42 us (31%)
  blocking collectives  8.29 us (30%)
  Pallas kernels  4.63 us (17%)
  waiting for transfers between devices  3.68 us (13%)
  other arithmetic  0.89 us (3%)
  between operations  0.7 us (3%)
    all_to_all x1, blocking collectives, exchange(): return lax.all_to_all(sent, axes, 0, 0, axis_index_groups=groups)  8.29 us
    all_to_all x1, starting transfers between devices, exchange(): return lax.all_to_all(sent, axes, 0, 0, axis_index_groups=groups)  7.25 us
    pallas_call x1, Pallas kernels, local(): pl.pallas_call(functools.partial(fetch, first, rows, adapters_here), out_...  2.55 us
    all_to_all x1, waiting for transfers between devices, exchange(): return lax.all_to_all(sent, axes, 0, 0, axis_index_groups=groups)  1.89 us
    pallas_call x1, Pallas kernels, local(): pl.pallas_call(functools.partial(pack, first, half_width), out_shape=jax....  1.41 us
    ppermute x1, waiting for transfers between devices, local(): squares += lax.ppermute(squares, 'tp', swap)  1.11 us
    ppermute x1, starting transfers between devices, local(): lax.ppermute(own_columns, 'tp', swap).reshape(requests, feature_count)  1.03 us
    convert_element_type x1, other arithmetic, local(): return (summed.astype(jnp.bfloat16), normed.astype(jnp.bfloat16))  0.69 us
  transfers between devices with their start and end apart: 4, of which 4 were waited for; matrix products, arithmetic and copies ran while one was open for 1% of the time, Pallas kernels for 11%

profile of v7, /device:TPU:0, one launch (start us, length us, event | category | flops | bytes accessed | tf_op | source)
XLA Modules:
  0.0 27.0 jit_solution(42501344488057562)
XLA Ops:
  0.6 1.4 %pack.1 = bf16[8,4,2048]{2,1,0:T(4,128)(2,1)} custom-call(bf16[4,4096]{1,0:T(4,128)(2,1)} %hidden_ref.1), custom_call_target="tpu_custom_call" | custom-call | tf_op jit(solution)/shard_map/pack/pallas_call | solution.py:140
  2.0 7.3 %all-to-all-start = ((bf16[8,4,2048]{2,1,0:T(4,128)(2,1)}), bf16[8,4,2048]{2,1,0:T(4,128)(2,1)S(1)}, u32[]{:S(2)}, u32[]{:S(2)}) async-start(bf16[8,4,2048]{2,1,0:T(4,128)(2,1)} %pack.1), calls=%async_computation | async-start | bytes 262144 | tf_op jit(solution)/shard_map/all_to_all | solution.py:134
  9.3 2.6 %fetch.1 = (bf16[512,2048]{1,0:T(8,128)(2,1)S(1)}, bf16[2,64,2048]{2,1,0:T(8,128)(2,1)S(1)}, bf16[2,64,2048]{2,1,0:T(8,128)(2,1)S(1)}, f32[32,128]{1,0:T(8,128)S(1)}) custom-call(s32[2]{0:T(128)} %ids_ref.1, s32[2,4]{1,0:T(2,128)} %slots_ref.1, bf16[512,2048]{1,0:T(8,128)(2,1)} %weight_ref.1, bf16[8,64,2048]{2,1,0:T(8,128)(2,1)} %down_ref.1, ...), custom_call_target="tpu_custom_call" | custom-call | bytes 2097152 | tf_op jit(solution)/shard_map/fetch/pallas_call | solution.py:152
  11.9 1.9 %all-to-all-done = bf16[8,4,2048]{2,1,0:T(4,128)(2,1)S(1)} async-done(((bf16[8,4,2048]{2,1,0:T(4,128)(2,1)}), bf16[8,4,2048]{2,1,0:T(4,128)(2,1)S(1)}, u32[]{:S(2)}, u32[]{:S(2)}) %all-to-all-start) | async-done | bytes 131104 | tf_op jit(solution)/shard_map/all_to_all | solution.py:134
  13.8 1.0 %collective-permute-start = (bf16[8,4,512]{2,1,0:T(4,128)(2,1)S(1)}, bf16[8,4,512]{2,1,0:T(4,128)(2,1)S(1)}, u32[]{:S(2)}, u32[]{:S(2)}) collective-permute-start(bf16[8,4,512]{2,1,0:T(4,128)(2,1)S(1)} %constant_dynamic-slice_fusion), channel_id=1, source_target_pairs={{0,1},{1,0},{2,3},{3,2},{4,5},{5,4},{6,7},{7,6},{8,9},{9,8},{10,11... | collective-permute-start | bytes 98312 | tf_op jit(solution)/shard_map/ppermute | solution.py:179
  14.8 0.3 convolution_bitcast_fusion.own_ref
  15.1 0.0 copy-start
  15.1 0.0 copy-start.1
  15.1 0.1 collective-permute-start.1
  15.2 0.4 %collective-permute-done = bf16[8,4,512]{2,1,0:T(4,128)(2,1)S(1)} collective-permute-done((bf16[8,4,512]{2,1,0:T(4,128)(2,1)S(1)}, bf16[8,4,512]{2,1,0:T(4,128)(2,1)S(1)}, u32[]{:S(2)}, u32[]{:S(2)}) %collective-permute-start) | collective-permute-done | bytes 32800 | tf_op jit(solution)/shard_map/ppermute | solution.py:179
  15.7 0.5 %project.1.projected_ref = f32[32,2048]{1,0:T(8,128)S(1)} custom-call(bf16[32,512]{1,0:T(8,128)(2,1)S(1)} %reshape.20.own_columns_ref, bf16[32,512]{1,0:T(8,128)(2,1)S(1)} %reshape.21.other_columns_ref, bf16[512,2048]{1,0:T(8,128)(2,1)S(1)} %get-tuple-element.6.weight_ref), custom_call_target="tpu_custom_call" | custom-call | flops 67108864 | bytes 2359296 | tf_op jit(solution)/shard_map/project/pallas_call | solution.py:185
  16.1 0.3 collective-permute-done.1.other_ref
  16.4 0.2 combine.1
  16.6 8.3 %all_to_all.10 = bf16[8,4,2048]{2,1,0:T(4,128)(2,1)S(1)} all-to-all(bf16[8,4,2048]{2,1,0:T(4,128)(2,1)S(1)} %combine.1), channel_id=1, replica_groups={{8,12,0,14,10,2,4,6},{9,13,1,15,11,3,5,7},{24,28,16,30,26,18,20,22},{25..., dimensions={0} | all-to-all | bytes 262144 | tf_op jit(solution)/shard_map/all_to_all | solution.py:134
  24.9 0.1 convert_reduce_fusion
  24.9 0.0 copy-done
  25.0 0.1 multiply_reduce_fusion
  25.1 0.1 collective-permute-start.2
  25.2 1.1 %collective-permute-done.2 = f32[4,1]{0,1:T(1,128)S(1)} collective-permute-done((f32[4,1]{0,1:T(1,128)S(1)}, f32[4,1]{0,1:T(1,128)S(1)}, u32[]{:S(2)}, u32[]{:S(2)}) %collective-permute-start.2) | collective-permute-done | bytes 48 | tf_op jit(solution)/shard_map/ppermute | solution.py:209
  26.3 0.0 copy-done.1
  26.3 0.7 %multiply_convert_fusion = (bf16[4,2048]{1,0:T(4,128)(2,1)}, bf16[4,2048]{1,0:T(4,128)(2,1)}) fusion(f32[2048]{0:T(1024)S(1)} %copy-done.1, f32[4]{0:T(128)S(1)} %rsqrt_bitcast_fusion, f32[4,2048]{1,0:T(4,128)S(1)} %convert_reduce_fusion, bf16[4,2048]{1,0:T(4,128)(2,1)S(1)} %copy-done), kind=kLoop, calls=%fused_computation.2 | loop fusion | flops 49152 | bytes 90128 | tf_op jit(solution)/shard_map/convert_element_type | solution.py:211
  (5 shorter events, 0.1 us)
Async XLA Ops:
  2.0 11.7 %all-to-all-start = ((bf16[8,4,2048]{2,1,0:T(4,128)(2,1)}), bf16[8,4,2048]{2,1,0:T(4,128)(2,1)S(1)}, u32[]{:S(2)}, u32[]{:S(2)}) async-start(bf16[8,4,2048]{2,1,0:T(4,128)(2,1)} %pack.1), calls=%async_computation | async-start | bytes 262144 | tf_op jit(solution)/shard_map/all_to_all | solution.py:134
  13.8 1.9 %collective-permute-start = (bf16[8,4,512]{2,1,0:T(4,128)(2,1)S(1)}, bf16[8,4,512]{2,1,0:T(4,128)(2,1)S(1)}, u32[]{:S(2)}, u32[]{:S(2)}) collective-permute-start(bf16[8,4,512]{2,1,0:T(4,128)(2,1)S(1)} %constant_dynamic-slice_fusion), channel_id=1, source_target_pairs={{0,1},{1,0},{2,3},{3,2},{4,5},{5,4},{6,7},{7,6},{8,9},{9,8},{10,11... | collective-permute-start | bytes 98312 | tf_op jit(solution)/shard_map/ppermute | solution.py:179
  15.1 9.8 %copy-start = (bf16[4,2048]{1,0:T(4,128)(2,1)S(1)}, bf16[4,2048]{1,0:T(4,128)(2,1)}, u32[]{:S(2)}) copy-start(bf16[4,2048]{1,0:T(4,128)(2,1)} %param.9) | copy-start | bytes 49156
  15.1 11.2 %copy-start.1 = (f32[2048]{0:T(1024)S(1)}, f32[2048]{0:T(1024)}, u32[]{:S(2)}) copy-start(f32[2048]{0:T(1024)} %param.13) | copy-start | bytes 24580
  15.1 1.2 %collective-permute-start.1 = (f32[32,128]{1,0:T(8,128)S(1)}, f32[32,128]{1,0:T(8,128)S(1)}, u32[]{:S(2)}, u32[]{:S(2)}) collective-permute-start(f32[32,128]{1,0:T(8,128)S(1)} %convolution_bitcast_fusion.own_ref), channel_id=1, source_target_pairs={{0,1},{1,0},{2,3},{3,2},{4,5},{5,4},{6,7},{7,6},{8,9},{9,8},{10,11... | collective-permute-start | bytes 49160 | tf_op jit(solution)/shard_map/ppermute | solution.py:184
  25.1 1.2 %collective-permute-start.2 = (f32[4,1]{0,1:T(1,128)S(1)}, f32[4,1]{0,1:T(1,128)S(1)}, u32[]{:S(2)}, u32[]{:S(2)}) collective-permute-start(f32[4,1]{0,1:T(1,128)S(1)} %bitcast.12), channel_id=1, source_target_pairs={{0,1},{1,0},{2,3},{3,2},{4,5},{5,4},{6,7},{7,6},{8,9},{9,8},{10,11... | collective-permute-start | bytes 56 | tf_op jit(solution)/shard_map/ppermute | solution.py:209
